TPU v7x, 512 devices: a whole 4x4x16 slice. The times are simulated.
512 devices in a mesh: tm: 32 (over x_lo, z), space: 16 (over y, x_hi, core).
Axes of the slice: x: 4 (x_hi: 2, x_lo: 2; x = x_hi * 2 + x_lo), y: 4, z: 16, core: 2. Of those that a mesh axis runs over, the one named last changes fastest.
Arguments:
- features: bfloat16 [64, 128, 80, 128], P('tm', 'space'), may hold values from -6 to 6
- norm_gain: float32 [128], replicated, may hold values from 0.1 to 1.9
- kernel: bfloat16 [3456, 256], P('space'), may hold values from -0.109375 to 0.109375
- cotangent: bfloat16 [64, 128, 80, 256], P('tm', 'space'), may hold values from -6 to 6
Outputs:
- decoded: bfloat16 [64, 128, 80, 256], P('tm', 'space')
- kernel_grad: float32 [3456, 256], P('space')
- input_grad: bfloat16 [64, 128, 80, 128], P('tm', 'space')
All inputs are finite; a program needn't handle non-finite values.
Results may differ from a plain program's by a relative error of at most 0.005.
Values may be sent and summed in bfloat16 or wider, within the bound.
No kernel may reach another device: no remote copies, remote signals or barrier semaphores. Data moves between devices by JAX's collectives and lax.ppermute only.
A program may use at most 128 MiB of HBM per device.

v0:
```python
import jax
import jax.numpy as jnp
from jax import lax
from jax.sharding import PartitionSpec as P

epsilon = 1e-06


def from_behind(block, axis, distance):
    devices = range(lax.axis_size(axis))
    route = [(i - distance, i) for i in devices if i - distance in devices]
    return lax.ppermute(block, axis, route)


def padded_2(block, sides, width):
    for axis, dim in sides:
        count = lax.axis_size(axis)
        forward = [(i, i + 1) for i in range(count - 1)]
        backward = [(target, source) for source, target in forward]
        low = lax.ppermute(
            lax.slice_in_dim(block, block.shape[dim] - width, None, axis=dim), axis, forward
        )
        high = lax.ppermute(lax.slice_in_dim(block, 0, width, axis=dim), axis, backward)
        block = jnp.concatenate([low, block, high], axis=dim)
    return block


def activate(values, norm_gain):
    mean_square = jnp.mean(values * values, axis=-1, keepdims=True)
    return jax.nn.silu(values * lax.rsqrt(mean_square + epsilon) * norm_gain)


def stack_taps(window, frames, rows, cols, flipped):
    pieces = []
    for frame_tap in range(3):
        for row_tap in range(3):
            for col_tap in range(3):
                first = 2 - frame_tap if flipped else frame_tap
                top = 2 - row_tap if flipped else row_tap
                left = 2 - col_tap if flipped else col_tap
                pieces.append(
                    window[first : first + frames, top : top + rows, left : left + cols, :]
                )
    return jnp.stack(pieces, axis=-1).reshape(frames * rows * cols, -1)


def widen(block):
    return jnp.pad(block, ((0, 0), (0, 0), (1, 1), (0, 0)))


def on_device(features, norm_gain, kernel, cotangent):
    frames, rows, cols, channels = features.shape
    outputs = cotangent.shape[3]
    values = features.astype(jnp.float32)
    activated = activate(values, norm_gain).astype(jnp.bfloat16)
    previous = from_behind(activated, "tm", 1)
    padded = widen(padded_2(jnp.concatenate([previous, activated], 0), (("space", 1),), 1))
    patches = stack_taps(padded, frames, rows, cols, False)
    kernel_full = lax.all_gather(kernel, "space", axis=0, tiled=True)
    decoded = jnp.dot(patches, kernel_full, preferred_element_type=jnp.float32).astype(jnp.bfloat16)
    decoded = decoded.reshape(frames, rows, cols, outputs)
    following = from_behind(cotangent, "tm", -1)
    grad_padded = widen(padded_2(jnp.concatenate([cotangent, following], 0), (("space", 1),), 1))
    grad_patches = stack_taps(grad_padded, frames, rows, cols, True)
    kernel_back = lax.all_gather(kernel, "space", axis=0, tiled=True)
    transposed = (
        kernel_back.reshape(channels, 27, outputs)
        .transpose(2, 1, 0)
        .reshape(outputs * 27, channels)
    )
    act_grad = jnp.dot(grad_patches, transposed, preferred_element_type=jnp.float32)
    again = activate(values, norm_gain).astype(jnp.bfloat16)
    earlier = from_behind(again, "tm", 1)
    padded_back = widen(padded_2(jnp.concatenate([earlier, again], 0), (("space", 1),), 1))
    patches_back = stack_taps(padded_back, frames, rows, cols, False)
    grad_rows = cotangent.reshape(frames * rows * cols, outputs)
    partial_grad = lax.dot_general(
        patches_back, grad_rows, (((0,), (0,)), ((), ())), preferred_element_type=jnp.float32
    )
    shard_grad = lax.psum_scatter(partial_grad, "space", scatter_dimension=0, tiled=True)
    kernel_grad = lax.psum(shard_grad, "tm")
    _, pull = jax.vjp(lambda inner: activate(inner, norm_gain), values)
    input_grad = pull(act_grad.reshape(frames, rows, cols, channels))[0].astype(jnp.bfloat16)
    return (decoded, kernel_grad, input_grad)


def solution(mesh):
    in_specs = (P("tm", "space", None, None), P(), P("space", None), P("tm", "space", None, None))
    out_specs = (P("tm", "space", None, None), P("space", None), P("tm", "space", None, None))
    return jax.shard_map(
        on_device, mesh=mesh, in_specs=in_specs, out_specs=out_specs, check_vma=False
    )
```

profile of v0, /device:TPU:16, one launch (start us, length us, event | category | flops | bytes accessed | tf_op | source)
XLA Modules:
  0.0 551.9 jit_solution(17993753514932180586)
XLA Ops:
  7.2 1.3 collective-permute-start.3
  8.6 1.1 constant_dynamic-update-slice_fusion.1
  9.7 1.3 fusion.19
  11.0 14.9 %collective-permute-done.3 = bf16[2,8,80,256]{3,2,1,0:T(8,128)(2,1)S(1)} collective-permute-done((bf16[2,8,80,256]{3,2,1,0:T(8,128)(2,1)}, bf16[2,8,80,256]{3,2,1,0:T(8,128)(2,1)S(1)}, u32[]{:S(2)}, u32[]{:S(2)}) %collective-permute-start.3) | collective-permute-done | bytes 655392 | tf_op jit(solution)/shard_map/ppermute | solution.py:12
  26.1 1.9 collective-permute-start.4
  28.0 6.0 %collective-permute-start.5 = (bf16[4,1,80,256]{3,2,1,0:T(8,128)(2,1)S(1)}, bf16[4,1,80,256]{3,2,1,0:T(8,128)(2,1)S(1)}, u32[]{:S(2)}, u32[]{:S(2)}) collective-permute-start(bf16[4,1,80,256]{3,2,1,0:T(8,128)(2,1)S(1)} %get-tuple-element.4), channel_id=1, source_target_pairs={{1,0},{2,1},{3,2},{4,3},{5,4},{6,5},{7,6},{8,7},{9,8},{10,9},{11,1... | collective-permute-start | bytes 491528 | tf_op jit(solution)/shard_map/ppermute | solution.py:23
  35.1 1.7 collective-permute-done.5
  40.7 1.2 fusion.61
  43.7 1.1 fusion.59
  46.6 1.1 fusion.57
  49.5 1.1 fusion.55
  52.5 1.1 fusion.52
  55.4 1.1 fusion.50
  58.4 1.1 fusion.46
  61.4 1.2 fusion.44
  64.3 12.4 %all-gather.2.cloned.1.call-done = bf16[3456,256]{1,0:T(8,128)(2,1)} async-done(((bf16[216,256]{1,0:T(8,128)(2,1)}), bf16[3456,256]{1,0:T(8,128)(2,1)}) %all-gather.2.cloned.1.call-update) | async-done | bytes 1769488 | tf_op jit(solution)/shard_map/all_gather | solution.py:59
  76.7 2.6 reshape.44
  79.3 3.0 copy.58
  82.3 11.5 %fusion.28 = (f32[2,8,80]{2,1,0:T(8,128)S(1)}, f32[2,8,80,128]{3,2,1,0:T(8,128)S(1)}) fusion(bf16[2,8,80,128]{3,2,1,0:T(8,128)(2,1)S(1)} %copy-done.2, f32[128]{0:T(128)S(1)} %copy-done.3, f32[2,8,80]{2,1,0:T(8,128)S(1)} %fusion.92, bf16[2,8,80,256,27]{3,2,4,1,0:T(8,128)(2,1)} %fusion.41, bf16[128,27,256]{0,2,1:T(8,128)(2,1)} %copy.58), kind=kOutput, calls=%fused_computation.49 | convolution fusion | flops 2267380480 | bytes 20457984 | tf_op jit(solution)/shard_map/dot_general | solution.py:71
  93.7 1.1 fusion.18
  94.9 3.5 collective-permute-start
  98.4 7.4 %collective-permute-done = bf16[2,8,80,128]{3,2,1,0:T(8,128)(2,1)S(1)} collective-permute-done((bf16[2,8,80,128]{3,2,1,0:T(8,128)(2,1)S(1)}, bf16[2,8,80,128]{3,2,1,0:T(8,128)(2,1)S(1)}, u32[]{:S(2)}, u32[]{:S(2)}) %collective-permute-start) | collective-permute-done | bytes 327712 | tf_op jit(solution)/shard_map/ppermute | solution.py:12
  105.8 1.9 collective-permute-start.1
  107.7 6.2 %collective-permute-start.2 = (bf16[4,1,80,128]{3,2,1,0:T(8,128)(2,1)S(1)}, bf16[4,1,80,128]{3,2,1,0:T(8,128)(2,1)S(1)}, u32[]{:S(2)}, u32[]{:S(2)}) collective-permute-start(bf16[4,1,80,128]{3,2,1,0:T(8,128)(2,1)S(1)} %get-tuple-element.8), channel_id=1, source_target_pairs={{1,0},{2,1},{3,2},{4,3},{5,4},{6,5},{7,6},{8,7},{9,8},{10,9},{11,1... | collective-permute-start | bytes 245768 | tf_op jit(solution)/shard_map/ppermute | solution.py:23
  113.9 1.8 collective-permute-done.2
  137.2 16.9 %copy.32 = bf16[2,8,80,128,27]{2,1,0,4,3:T(8,128)(2,1)} copy(bf16[2,8,80,128,27]{3,2,1,0,4:T(8,128)(2,1)} %fusion.66) | data formatting | bytes 17694720 | tf_op jit(solution)/shard_map/stack | solution.py:44
  154.1 22.5 %reshape.41 = bf16[1280,3456]{0,1:T(8,128)(2,1)} reshape(bf16[2,8,80,128,27]{2,1,0,4,3:T(8,128)(2,1)} %copy.32) | data formatting | bytes 17694720 | tf_op jit(solution)/shard_map/reshape | solution.py:44
  176.7 7.9 %fusion.94 = f32[3456,256]{1,0:T(8,128)} fusion(bf16[1280,3456]{0,1:T(8,128)(2,1)} %reshape.41, bf16[1280,256]{1,0:T(8,128)(2,1)S(1)} %bitcast.287), kind=kOutput, calls=%fused_computation.169 | convolution fusion | flops 2264924160 | bytes 13041664 | tf_op jit(solution)/shard_map/dot_general | solution.py:77
  184.6 104.5 %reduce-scatter.2.cloned.1.call-done = f32[216,256]{1,0:T(8,128)} async-done(((f32[3456,256]{1,0:T(8,128)}), f32[216,256]{1,0:T(8,128)}) %reduce-scatter.2.cloned.1.call-update) | async-done | bytes 221200 | tf_op jit(solution)/shard_map/reduce_scatter | solution.py:80
  289.1 6.9 %convolution_convert_fusion = bf16[1280,256]{1,0:T(8,128)(2,1)} fusion(bf16[1280,3456]{0,1:T(8,128)(2,1)} %reshape.41, bf16[3456,256]{1,0:T(8,128)(2,1)S(1)} %copy-done.1), kind=kOutput, calls=%fused_computation.5 | convolution fusion | flops 2265251840 | bytes 11272192 | tf_op jit(solution)/shard_map/dot_general | solution.py:60
  296.0 247.6 %all-reduce.4.cloned.1.call-done = f32[216,256]{1,0:T(8,128)} async-done(((f32[216,256]{1,0:T(8,128)}), f32[216,256]{1,0:T(8,128)}) %all-reduce.4.cloned.1.call-update) | async-done | bytes 221200 | tf_op jit(solution)/shard_map/psum | solution.py:81
  543.7 1.6 copy.115
  (70 shorter events, 41.2 us)
Async XLA Ops:
  7.2 69.6 %all-gather.2.cloned.1.call-start = ((), (), s32[]{:S(2)}) async-start(), calls=%async_computation.1 | async-start | bytes 1880064 | tf_op jit(solution)/shard_map/all_gather | solution.py:59
  7.2 18.8 %collective-permute-start.3 = (bf16[2,8,80,256]{3,2,1,0:T(8,128)(2,1)}, bf16[2,8,80,256]{3,2,1,0:T(8,128)(2,1)S(1)}, u32[]{:S(2)}, u32[]{:S(2)}) collective-permute-start(bf16[2,8,80,256]{3,2,1,0:T(8,128)(2,1)} %param.7), channel_id=1, source_target_pairs={{16,0},{32,16},{48,32},{64,48},{80,64},{96,80},{112,96},{128,112},... | collective-permute-start | bytes 1966088 | tf_op jit(solution)/shard_map/ppermute | solution.py:12
  8.5 280.5 %reduce-scatter.2.cloned.1.call-start = ((), (), s32[]{:S(2)}) async-start(), calls=%async_computation.2 | async-start | bytes 3760128 | tf_op jit(solution)/shard_map/reduce_scatter | solution.py:80
  26.1 9.1 %collective-permute-start.4 = (bf16[4,1,80,256]{3,2,1,0:T(8,128)(2,1)S(1)}, bf16[4,1,80,256]{3,2,1,0:T(8,128)(2,1)S(1)}, u32[]{:S(2)}, u32[]{:S(2)}) collective-permute-start(bf16[4,1,80,256]{3,2,1,0:T(8,128)(2,1)S(1)} %get-tuple-element.3), channel_id=1, source_target_pairs={{0,1},{1,2},{2,3},{3,4},{4,5},{5,6},{6,7},{7,8},{8,9},{9,10},{10,1... | collective-permute-start | bytes 491528 | tf_op jit(solution)/shard_map/ppermute | solution.py:20
  28.0 8.9 %collective-permute-start.5 = (bf16[4,1,80,256]{3,2,1,0:T(8,128)(2,1)S(1)}, bf16[4,1,80,256]{3,2,1,0:T(8,128)(2,1)S(1)}, u32[]{:S(2)}, u32[]{:S(2)}) collective-permute-start(bf16[4,1,80,256]{3,2,1,0:T(8,128)(2,1)S(1)} %get-tuple-element.4), channel_id=1, source_target_pairs={{1,0},{2,1},{3,2},{4,3},{5,4},{6,5},{7,6},{8,7},{9,8},{10,9},{11,1... | collective-permute-start | bytes 491528 | tf_op jit(solution)/shard_map/ppermute | solution.py:23
  47.7 11.9 %copy-start = (bf16[2,8,80,256]{3,2,1,0:T(8,128)(2,1)S(1)}, bf16[2,8,80,256]{3,2,1,0:T(8,128)(2,1)}, u32[]{:S(2)}) copy-start(bf16[2,8,80,256]{3,2,1,0:T(8,128)(2,1)} %param.7) | copy-start | bytes 1966084
  57.5 24.8 %copy-start.2 = (bf16[2,8,80,128]{3,2,1,0:T(8,128)(2,1)S(1)}, bf16[2,8,80,128]{3,2,1,0:T(8,128)(2,1)}, u32[]{:S(2)}) copy-start(bf16[2,8,80,128]{3,2,1,0:T(8,128)(2,1)} %param.4) | copy-start | bytes 983044
  57.5 24.8 %copy-start.3 = (f32[128]{0:T(128)S(1)}, f32[128]{0:T(128)}, u32[]{:S(2)}) copy-start(f32[128]{0:T(128)} %param.5) | copy-start | bytes 1540
  94.9 10.8 %collective-permute-start = (bf16[2,8,80,128]{3,2,1,0:T(8,128)(2,1)S(1)}, bf16[2,8,80,128]{3,2,1,0:T(8,128)(2,1)S(1)}, u32[]{:S(2)}, u32[]{:S(2)}) collective-permute-start(bf16[2,8,80,128]{3,2,1,0:T(8,128)(2,1)S(1)} %get-tuple-element.10), channel_id=1, source_target_pairs={{0,16},{16,32},{32,48},{48,64},{64,80},{80,96},{96,112},{112,128},... | collective-permute-start | bytes 983048 | tf_op jit(solution)/shard_map/ppermute | solution.py:12
  105.8 8.2 %collective-permute-start.1 = (bf16[4,1,80,128]{3,2,1,0:T(8,128)(2,1)S(1)}, bf16[4,1,80,128]{3,2,1,0:T(8,128)(2,1)S(1)}, u32[]{:S(2)}, u32[]{:S(2)}) collective-permute-start(bf16[4,1,80,128]{3,2,1,0:T(8,128)(2,1)S(1)} %get-tuple-element.7), channel_id=1, source_target_pairs={{0,1},{1,2},{2,3},{3,4},{4,5},{5,6},{6,7},{7,8},{8,9},{9,10},{10,1... | collective-permute-start | bytes 245768 | tf_op jit(solution)/shard_map/ppermute | solution.py:20
  107.7 8.1 %collective-permute-start.2 = (bf16[4,1,80,128]{3,2,1,0:T(8,128)(2,1)S(1)}, bf16[4,1,80,128]{3,2,1,0:T(8,128)(2,1)S(1)}, u32[]{:S(2)}, u32[]{:S(2)}) collective-permute-start(bf16[4,1,80,128]{3,2,1,0:T(8,128)(2,1)S(1)} %get-tuple-element.8), channel_id=1, source_target_pairs={{1,0},{2,1},{3,2},{4,3},{5,4},{6,5},{7,6},{8,7},{9,8},{10,9},{11,1... | collective-permute-start | bytes 245768 | tf_op jit(solution)/shard_map/ppermute | solution.py:23
  176.7 112.4 %copy-start.1 = (bf16[3456,256]{1,0:T(8,128)(2,1)S(1)}, bf16[3456,256]{1,0:T(8,128)(2,1)}, u32[]{:S(2)}) copy-start(bf16[3456,256]{1,0:T(8,128)(2,1)} %all-gather.2.cloned.1.call-done) | copy-start | bytes 5308420
  184.5 359.1 %all-reduce.4.cloned.1.call-start = ((), (), s32[]{:S(2)}) async-start(), calls=%async_computation.3 | async-start | bytes 442368 | tf_op jit(solution)/shard_map/psum | solution.py:81
Sparse Core Ops, SparseCore 0:
  11.3 65.4 all-gather.1
  184.7 104.3 reduce-scatter.1
  292.0 251.6 all-reduce.3
where the time goes:
time: 554 us; the launch traced here: 552 us
  waiting for transfers between devices  391 us (71%)
  local copies, waits for them, and re-layouts  89 us (16%)
  matrix products  26.3 us (5%)
  starting transfers between devices  21 us (4%)
  between operations  13.9 us (3%)
  other arithmetic  10.2 us (2%)
    psum x1, waiting for transfers between devices, on_device(): kernel_grad = lax.psum(shard_grad, 'tm')  248 us
    reduce_scatter x1, waiting for transfers between devices, on_device(): lax.psum_scatter(partial_grad, 'space', scatter_dimension=0, tiled=True)  104 us
    unnamed x55, local copies, waits for them, and re-layouts  42.2 us
    reshape x1, local copies, waits for them, and re-layouts, stack_taps(): return jnp.stack(pieces, axis=-1).reshape(frames * rows * cols, -1)  22.5 us
    ppermute x2, waiting for transfers between devices, from_behind(): return lax.ppermute(block, axis, route)  22.3 us
    another operation x3, local copies, waits for them, and re-layouts, stack_taps(): return jnp.stack(pieces, axis=-1).reshape(frames * rows * cols, -1)  18.7 us
    all_gather x1, waiting for transfers between devices, on_device(): kernel_full = lax.all_gather(kernel, 'space', axis=0, tiled=True)  12.4 us
    ppermute x2, starting transfers between devices, padded_2(): lax.ppermute(lax.slice_in_dim(block, 0, width, axis=dim), axis, backward)  12.3 us
  transfers between devices with their start and end apart: 9, of which 8 were waited for; matrix products, arithmetic and copies ran while one was open for 7% of the time, Pallas kernels for 0%

commit v1 on v0

v1 whole, which is shorter than its diff:
```python
import jax
import jax.numpy as jnp
from jax import lax
from jax.experimental import pallas as pl
from jax.experimental.pallas import tpu as pltpu
from jax.sharding import Mesh, PartitionSpec as P

epsilon = 1e-06
F32 = jnp.float32
BF16 = jnp.bfloat16
TM = ("xl", "z1", "z0")
SPACE = ("y", "xh", "co")
SIZES = (2, 4, 4, 4, 2, 2)
AXES = TM + SPACE
TMS, SPACES = 32, 16


def shift(block, target):
    route = []
    for t in range(TMS):
        for s in range(SPACES):
            u, v = target(t, s)
            if 0 <= u < TMS and 0 <= v < SPACES:
                route.append((t * SPACES + s, u * SPACES + v))
    return lax.ppermute(block, AXES, route)


def beside(block):
    cols = block.shape[1]
    col = lax.broadcasted_iota(jnp.int32, block.shape, 1)
    left = jnp.where(col == 0, 0.0, pltpu.roll(block, 1, 1))
    right = jnp.where(col == cols - 1, 0.0, pltpu.roll(block, cols - 1, 1))
    return jnp.concatenate([left, block, right], axis=-1).astype(BF16)


def activated(block, gain):
    frames, rows, cols, channels = block.shape
    v = block.reshape(frames * rows, cols, channels).astype(F32)
    z = v * lax.rsqrt(jnp.mean(v * v, axis=-1, keepdims=True) + epsilon) * gain
    return z / (1.0 + jnp.exp(-z))


def gradient(act, pad):
    frames = act.shape[0]
    rows = act.reshape(frames * 640, 384)
    shifted = [pad[:, 2 - b : 10 - b].reshape(frames * 640, 256) for b in range(3)]
    return lax.dot_general(
        rows,
        jnp.concatenate(shifted, axis=-1),
        (((0,), (0,)), ((), ())),
        preferred_element_type=F32,
    )


def prepare_body(own, gain, cot, act, held):
    g = gain[...].reshape(1, 1, 128)
    act[...] = beside(activated(own[...], g)).reshape(2, 8, 80, 384)
    held[...] = cot[...]


def own_grad_body(act, cot, top, low, pad, edges, part):
    pad[:, 1:9] = cot[...]
    edges[:, 0:1] = top[...]
    edges[:, 1:2] = low[...]
    pad[:, 0:1] = top[...]
    pad[:, 9:10] = low[...]
    part[0] = gradient(act[0:1], pad[1:2])
    part[1] = gradient(act[...], pad[...])


def rest_grad_body(
    core, prev, gain, own_act, pad, part, act, first, last, keep, send, total
):
    g = gain[...].reshape(1, 1, 128)
    a32 = activated(prev[...], g)
    act[...] = beside(a32).reshape(2, 8, 80, 384)
    first[0:2] = act[:, 0:1, :, 128:256]
    last[0:2] = act[:, 7:8, :, 128:256]
    first[2:4] = own_act[:, 0:1, :, 128:256]
    last[2:4] = own_act[:, 7:8, :, 128:256]
    total[0] = gradient(act[...], pad[...])
    total[1] = part[0] + gradient(act[1:2], pad[0:1])

    def tap(index):
        a, b, e = index // 9, index // 3 % 3, index % 3
        ref = part.at[1] if a == 2 else total.at[a]
        return ref, 128 * e, 256 * b

    def pack(even, odd):
        for pair in range(14):
            for chip in range(8):
                for out, parity in ((even, 0), (odd, 1)):
                    blocks = []
                    for index in (2 * pair, min(2 * pair + 1, 26)):
                        ref, row, col = tap(index)
                        row = row + 16 * chip + 8 * parity
                        blocks.append(ref[row : row + 8, col : col + 256])
                    if pair == 13:
                        blocks[1] = jnp.zeros_like(blocks[1])
                    both = jnp.concatenate(blocks, axis=0).astype(BF16)
                    out[chip, 16 * pair : 16 * pair + 16] = both

    @pl.when(core[0] == 0)
    def _():
        pack(keep, send)

    @pl.when(core[0] != 0)
    def _():
        pack(send, keep)


VMEM = pl.BlockSpec(memory_space=pltpu.VMEM)
SMEM = pl.BlockSpec(memory_space=pltpu.SMEM)


def prepare(own, gain, cot):
    return pl.pallas_call(
        prepare_body,
        out_shape=(
            jax.ShapeDtypeStruct((2, 8, 80, 384), BF16),
            jax.ShapeDtypeStruct((2, 8, 80, 256), BF16),
        ),
        in_specs=[VMEM] * 3,
        out_specs=(VMEM,) * 2,
        compiler_params=pltpu.CompilerParams(vmem_limit_bytes=8 << 20),
        name="prepare",
    )(own, gain, cot)


def own_grad(act, cot, top, low):
    return pl.pallas_call(
        own_grad_body,
        out_shape=(
            jax.ShapeDtypeStruct((2, 10, 80, 256), BF16),
            jax.ShapeDtypeStruct((2, 2, 80, 256), BF16),
            jax.ShapeDtypeStruct((2, 384, 768), F32),
        ),
        in_specs=[VMEM] * 4,
        out_specs=(VMEM,) * 3,
        compiler_params=pltpu.CompilerParams(vmem_limit_bytes=10 << 20),
        cost_estimate=pl.CostEstimate(
            flops=1280 * 3456 * 256, bytes_accessed=6 << 20, transcendentals=0
        ),
        name="own_grad",
    )(act, cot, top, low)


def rest_grad(core, prev, gain, own_act, pad, part):
    return pl.pallas_call(
        rest_grad_body,
        out_shape=(
            jax.ShapeDtypeStruct((2, 8, 80, 384), BF16),
            jax.ShapeDtypeStruct((4, 1, 80, 128), BF16),
            jax.ShapeDtypeStruct((4, 1, 80, 128), BF16),
            jax.ShapeDtypeStruct((8, 224, 256), BF16),
            jax.ShapeDtypeStruct((8, 224, 256), BF16),
        ),
        in_specs=[SMEM] + [VMEM] * 5,
        out_specs=(VMEM,) * 5,
        scratch_shapes=[pltpu.VMEM((2, 384, 768), F32)],
        compiler_params=pltpu.CompilerParams(vmem_limit_bytes=12 << 20),
        cost_estimate=pl.CostEstimate(
            flops=1280 * 3456 * 256, bytes_accessed=6 << 20, transcendentals=1 << 18
        ),
        name="rest_grad",
    )(core, prev, gain, own_act, pad, part)


def call(body, name, out_shape, args, specs=None, scratch=()):
    return pl.pallas_call(
        body,
        out_shape=out_shape,
        in_specs=specs or [VMEM] * len(args),
        out_specs=VMEM,
        scratch_shapes=scratch,
        compiler_params=pltpu.CompilerParams(vmem_limit_bytes=6 << 20),
        name=name,
    )(*args)


def add_cores(keep, got):
    def body(keep_ref, got_ref, out_ref):
        out_ref[...] = (keep_ref[...].astype(F32) + got_ref[...].astype(F32)).astype(BF16)

    shape = jax.ShapeDtypeStruct(keep.shape, BF16)
    return call(body, "add_cores", shape, (keep, got))


def add_chips(rows):
    def body(rows_ref, out_ref):
        total = rows_ref[0].astype(F32)
        for chip in range(1, 8):
            total = total + rows_ref[chip].astype(F32)
        for side in range(2):
            for quarter in range(4):
                block = total[56 * quarter : 56 * quarter + 56, 128 * side : 128 * side + 128]
                out_ref[4 * side + quarter] = block

    shape = jax.ShapeDtypeStruct((8, 56, 128), F32)
    return call(body, "add_chips", shape, (rows,))


def add_parts(parts):
    def body(parts_ref, out_ref):
        out_ref[...] = jnp.sum(parts_ref[...], axis=0)

    return call(body, "add_parts", jax.ShapeDtypeStruct(parts.shape[1:], F32), (parts,))


def add_far(own, near, far, farthest):
    def body(own_ref, near_ref, far_ref, farthest_ref, out_ref):
        total = (own_ref[...] + near_ref[...]) + (far_ref[...] + farthest_ref[...])
        out_ref[...] = jnp.broadcast_to(total, (8, 56, 128))

    shape = jax.ShapeDtypeStruct((8, 56, 128), F32)
    return call(body, "add_far", shape, (own, near, far, farthest))


def finish(whole):
    def body(whole_ref, out_ref, side_ref):
        for side in range(2):
            for tap in range(27):
                row = 8 * tap
                block = whole_ref[4 * side + row // 56, row % 56 : row % 56 + 8]
                side_ref[side, pl.ds(tap, 8, stride=27), :] = block
            out_ref[:, 128 * side : 128 * side + 128] = side_ref[side]

    shape = jax.ShapeDtypeStruct((216, 256), F32)
    scratch = (pltpu.VMEM((2, 216, 128), F32),)
    return call(body, "finish", shape, (whole,), None, scratch)


def outputs_body(
    pieces,
    prev_act,
    own_act,
    top,
    low,
    own,
    pad,
    next_cot,
    next_edges,
    gain,
    dec,
    ing,
    kern,
    raw,
    edge,
):
    for chip in range(8):
        for side in range(2):
            columns = slice(128 * side, 128 * side + 128)
            for half in range(2):
                raw[side, half] = pieces[2 * chip + half, :, columns].astype(F32)
            for tap in range(27):
                rows = [raw[side, half, pl.ds(tap, 8, stride=27), :] for half in range(2)]
                rows = jnp.concatenate(rows, axis=0).astype(BF16)
                kern[tap, 16 * chip : 16 * chip + 16, columns] = rows
    edge[0] = beside(top[...].reshape(4, 80, 128).astype(F32))
    edge[1] = beside(low[...].reshape(4, 80, 128).astype(F32))

    def act_rows(frame, at):
        act, index = (prev_act, frame) if frame < 2 else (own_act, frame - 2)
        if at < 0:
            rows = jnp.concatenate([edge[0, frame : frame + 1], act[index, 0:3]], axis=0)
        elif at > 4:
            rows = jnp.concatenate([act[index, 5:8], edge[1, frame : frame + 1]], axis=0)
        else:
            rows = act[index, at : at + 4]
        return rows.reshape(320, 384)

    for t in range(2):
        for half in range(2):
            patches = [
                act_rows(t + a, 4 * half + b - 1) for a in range(3) for b in range(3)
            ]
            out = jnp.dot(
                jnp.concatenate(patches, axis=-1),
                kern[...].reshape(3456, 256),
                preferred_element_type=F32,
            )
            dec[t, 4 * half : 4 * half + 4] = out.astype(BF16).reshape(4, 80, 256)

    def cot_rows(frame, at):
        if frame < 2:
            return pad[frame, at + 1 : at + 5].reshape(320, 256)
        cot, edges = next_cot[frame - 2], next_edges[frame - 2]
        if at < 0:
            rows = jnp.concatenate([edges[0:1], cot[0:3]], axis=0)
        elif at > 4:
            rows = jnp.concatenate([cot[5:8], edges[1:2]], axis=0)
        else:
            rows = cot[at : at + 4]
        return rows.reshape(320, 256)

    g = gain[...].reshape(1, 1, 128)
    for s in range(2):
        for half in range(2):
            sums = jnp.zeros((320, 384), F32)
            for a in range(3):
                for b in range(3):
                    window = cot_rows(s + 2 - a, 4 * half + 1 - b)
                    weights = kern[9 * a + 3 * b : 9 * a + 3 * b + 3].reshape(384, 256)
                    sums = sums + lax.dot_general(
                        window, weights, (((1,), (1,)), ((), ())), preferred_element_type=F32
                    )
            sums = sums.reshape(4, 80, 384)
            left, mid, right = sums[..., :128], sums[..., 128:256], sums[..., 256:]
            col = lax.broadcasted_iota(jnp.int32, mid.shape, 1)
            grad = mid + jnp.where(col == 79, 0.0, pltpu.roll(left, 79, 1))
            grad = grad + jnp.where(col == 0, 0.0, pltpu.roll(right, 1, 1))
            v = own[s, 4 * half : 4 * half + 4].astype(F32)
            scale = lax.rsqrt(jnp.mean(v * v, axis=-1, keepdims=True) + epsilon)
            normed = v * scale
            z = normed * g
            gate = 1.0 / (1.0 + jnp.exp(-z))
            dn = grad * (gate * (1.0 + z * (1.0 - gate))) * g
            out = scale * (dn - normed * jnp.mean(dn * normed, axis=-1, keepdims=True))
            ing[s, 4 * half : 4 * half + 4] = out.astype(BF16)


def outputs(pieces, prev_act, own_act, top, low, own, pad, next_cot, next_edges, gain):
    return pl.pallas_call(
        outputs_body,
        out_shape=(
            jax.ShapeDtypeStruct((2, 8, 80, 256), BF16),
            jax.ShapeDtypeStruct((2, 8, 80, 128), BF16),
        ),
        in_specs=[VMEM] * 10,
        out_specs=(VMEM,) * 2,
        scratch_shapes=[
            pltpu.VMEM((27, 128, 256), BF16),
            pltpu.VMEM((2, 2, 216, 128), F32),
            pltpu.VMEM((2, 4, 80, 384), BF16),
        ],
        compiler_params=pltpu.CompilerParams(vmem_limit_bytes=20 << 20),
        cost_estimate=pl.CostEstimate(
            flops=4 * 1280 * 3456 * 256, bytes_accessed=8 << 20, transcendentals=1 << 18
        ),
        name="outputs",
    )(pieces, prev_act, own_act, top, low, own, pad, next_cot, next_edges, gain)


def on_device(features, norm_gain, kernel, cotangent):
    core = lax.axis_index("co").reshape(1)
    prev = shift(features, lambda t, s: (t + 1, s))
    top = shift(cotangent[:, 7:], lambda t, s: (t, s + 1))
    low = shift(cotangent[:, :1], lambda t, s: (t, s - 1))
    pieces = lax.all_gather(kernel, SPACE, axis=0)
    next_cot = shift(cotangent, lambda t, s: (t - 1, s))
    own_act, held = prepare(features, norm_gain, cotangent)
    pad, edges, part = own_grad(own_act, held, top, low)
    prev, next_cot = lax.optimization_barrier((prev, next_cot))
    prev_act, first, last, keep, send = rest_grad(core, prev, norm_gain, own_act, pad, part)
    next_edges = shift(edges, lambda t, s: (t - 1, s))
    act_top = shift(last, lambda t, s: (t, s + 1))
    act_low = shift(first, lambda t, s: (t, s - 1))
    both = add_cores(keep, shift(send, lambda t, s: (t, s ^ 1)))
    rows = lax.all_to_all(both, ("y", "xh"), 0, 0, tiled=True)
    rows, next_edges, act_top, act_low = lax.optimization_barrier(
        (rows, next_edges, act_top, act_low)
    )
    parts = add_chips(rows)
    part = add_parts(lax.all_to_all(parts, ("xl", "z0"), 0, 0, tiled=True))
    near, far, farthest = [shift(part, lambda t, s: (t ^ step, s)) for step in (4, 8, 12)]
    decoded, input_grad = outputs(
        pieces,
        prev_act,
        own_act,
        act_top,
        act_low,
        features,
        pad,
        next_cot,
        next_edges,
        norm_gain,
    )
    far, decoded, input_grad = lax.optimization_barrier((far, decoded, input_grad))
    whole = add_far(part, near, far, farthest)
    whole = lax.all_to_all(whole, ("xl", "z0"), 0, 0, tiled=True)
    kernel_grad = finish(whole)
    return (decoded, kernel_grad, input_grad)


def solution(mesh):
    fine = Mesh(mesh.devices.reshape(SIZES), AXES)
    split = P(TM, SPACE, None, None)
    rows = P(SPACE, None)
    return jax.shard_map(
        on_device,
        mesh=fine,
        in_specs=(split, P(), rows, split),
        out_specs=(split, rows, split),
        check_vma=False,
    )
```

time: 554 us -> 138 us (0.25)
  the two profiles are of different devices: /device:TPU:16 before, /device:TPU:8 now
where the time goes in v1:
time: 138 us; the launch traced here: 137 us
  starting transfers between devices  56.8 us (41%)
  blocking collectives  33.8 us (24%)
  Pallas kernels  14.9 us (11%)
  between operations  14.2 us (10%)
  local copies, waits for them, and re-layouts  9.22 us (7%)
  waiting for transfers between devices  8.04 us (6%)
    ppermute x11, starting transfers between devices, shift(): return lax.ppermute(block, AXES, route)  50.1 us
    all_to_all x1, blocking collectives, on_device(): part = add_parts(lax.all_to_all(parts, ('xl', 'z0'), 0, 0, tiled=True))  23.1 us
    all_to_all x1, blocking collectives, on_device(): whole = lax.all_to_all(whole, ('xl', 'z0'), 0, 0, tiled=True)  10.7 us
    unnamed x22, local copies, waits for them, and re-layouts  8.28 us
    pallas_call x1, Pallas kernels, outputs(): pl.pallas_call(outputs_body, out_shape=(jax.ShapeDtypeStruct((2, 8, 80, 2...  8.09 us
    ppermute x11, waiting for transfers between devices, shift(): return lax.ppermute(block, AXES, route)  7.23 us
    all_to_all x1, starting transfers between devices, on_device(): rows = lax.all_to_all(both, ('y', 'xh'), 0, 0, tiled=True)  6.61 us
    pallas_call x1, Pallas kernels, rest_grad(): pl.pallas_call(rest_grad_body, out_shape=(jax.ShapeDtypeStruct((2, 8, 80,...  2.83 us
  transfers between devices with their start and end apart: 13, of which 3 were waited for; matrix products, arithmetic and copies ran while one was open for 1% of the time, Pallas kernels for 10%

profile of v1, /device:TPU:8, one launch (start us, length us, event | category | flops | bytes accessed | tf_op | source)
XLA Modules:
  0.0 137.0 jit_solution(13156619824690388666)
XLA Ops:
  7.2 0.7 all-gather.3.cloned.1.call-update
  7.9 1.3 collective-permute-start.1
  9.2 4.6 %collective-permute-start = (bf16[2,8,80,128]{3,2,1,0:T(8,128)(2,1)}, bf16[2,8,80,128]{3,2,1,0:T(8,128)(2,1)S(1)}, u32[]{:S(2)}, u32[]{:S(2)}) collective-permute-start(bf16[2,8,80,128]{3,2,1,0:T(8,128)(2,1)} %own.3), channel_id=1, source_target_pairs={{0,16},{1,17},{2,18},{3,19},{4,20},{5,21},{6,22},{7,23},{8,24},{9,... | collective-permute-start | bytes 983048 | tf_op jit(solution)/shard_map/ppermute | solution.py:25
  13.8 0.9 fusion
  14.7 1.9 %collective-permute-start.2 = (bf16[2,1,80,256]{3,2,1,0:T(8,128)(2,1)S(1)}, bf16[2,1,80,256]{3,2,1,0:T(8,128)(2,1)S(1)}, u32[]{:S(2)}, u32[]{:S(2)}) collective-permute-start(bf16[2,1,80,256]{3,2,1,0:T(8,128)(2,1)S(1)} %get-tuple-element.46), channel_id=1, source_target_pairs={{0,1},{1,2},{2,3},{3,4},{4,5},{5,6},{6,7},{7,8},{8,9},{9,10},{10,1... | collective-permute-start | bytes 245768 | tf_op jit(solution)/shard_map/ppermute | solution.py:25
  16.7 6.0 %collective-permute-start.3 = (bf16[2,1,80,256]{3,2,1,0:T(8,128)(2,1)S(1)}, bf16[2,1,80,256]{3,2,1,0:T(8,128)(2,1)S(1)}, u32[]{:S(2)}, u32[]{:S(2)}) collective-permute-start(bf16[2,1,80,256]{3,2,1,0:T(8,128)(2,1)S(1)} %get-tuple-element.45), channel_id=1, source_target_pairs={{1,0},{2,1},{3,2},{4,3},{5,4},{6,5},{7,6},{8,7},{9,8},{10,9},{11,1... | collective-permute-start | bytes 245768 | tf_op jit(solution)/shard_map/ppermute | solution.py:25
  22.7 1.1 copy-done
  23.8 1.0 copy-done.1
  24.8 0.7 copy-done.3
  25.4 0.5 prepare.1
  25.9 0.8 copy-done.8
  26.8 1.1 copy-done.9
  27.9 1.4 %own_grad.1 = (bf16[2,10,80,256]{3,2,1,0:T(8,128)(2,1)S(1)}, bf16[2,2,80,256]{3,2,1,0:T(8,128)(2,1)S(1)}, f32[2,384,768]{2,1,0:T(8,128)S(1)}) custom-call(bf16[2,8,80,384]{3,2,1,0:T(8,128)(2,1)S(1)} %get-tuple-element.25.act.own_act, bf16[2,8,80,256]{3,2,1,0:T(8,128)(2,1)S(1)} %copy-done.9, bf16[2,1,80,256]{3,2,1,0:T(8,128)(2,1)S(1)} %collective-permute-done.2.top, ...), custom_call_target="tpu_custom_call" | custom-call | flops 1132462080 | bytes 6291456 | tf_op jit(solution)/shard_map/own_grad/pallas_call | solution.py:131
  29.3 2.8 %rest_grad.1 = (bf16[2,8,80,384]{3,2,1,0:T(8,128)(2,1)S(1)}, bf16[4,1,80,128]{3,2,1,0:T(8,128)(2,1)S(1)}, bf16[4,1,80,128]{3,2,1,0:T(8,128)(2,1)}, bf16[8,224,25...) custom-call(s32[1]{0:T(128)} %bitcast.core, bf16[2,8,80,128]{3,2,1,0:T(8,128)(2,1)S(1)} %collective-permute-done.prev, ...), custom_call_target="tpu_custom_call" | custom-call | flops 1132462080 | bytes 6291456 | tf_op jit(solution)/shard_map/rest_grad/pallas_call | solution.py:149
  32.2 1.0 copy-done.6
  33.1 2.2 %collective-permute-start.4 = (bf16[8,224,256]{2,1,0:T(8,128)(2,1)S(1)}, bf16[8,224,256]{2,1,0:T(8,128)(2,1)S(1)}, u32[]{:S(2)}, u32[]{:S(2)}) collective-permute-start(bf16[8,224,256]{2,1,0:T(8,128)(2,1)S(1)} %get-tuple-element.30), channel_id=1, source_target_pairs={{0,1},{1,0},{2,3},{3,2},{4,5},{5,4},{6,7},{7,6},{8,9},{9,8},{10,11... | collective-permute-start | bytes 2752520 | tf_op jit(solution)/shard_map/ppermute | solution.py:25
  35.3 2.2 %collective-permute-done.4.got_ref = bf16[8,224,256]{2,1,0:T(8,128)(2,1)S(1)} collective-permute-done((bf16[8,224,256]{2,1,0:T(8,128)(2,1)S(1)}, bf16[8,224,256]{2,1,0:T(8,128)(2,1)S(1)}, u32[]{:S(2)}, u32[]{:S(2)}) %collective-permute-start.4) | collective-permute-done | bytes 917536 | tf_op jit(solution)/shard_map/ppermute | solution.py:25
  37.5 1.2 add_cores.1
  38.6 6.6 %all-to-all-start = ((bf16[8,224,256]{2,1,0:T(8,128)(2,1)}), bf16[8,224,256]{2,1,0:T(8,128)(2,1)S(1)}, u32[]{:S(2)}, u32[]{:S(2)}) async-start(bf16[8,224,256]{2,1,0:T(8,128)(2,1)} %add_cores.1), calls=%async_computation | async-start | bytes 1835008 | tf_op jit(solution)/shard_map/all_to_all | solution.py:359
  45.3 1.3 collective-permute-start.5
  46.6 1.9 %collective-permute-start.6 = (bf16[4,1,80,128]{3,2,1,0:T(8,128)(2,1)}, bf16[4,1,80,128]{3,2,1,0:T(8,128)(2,1)S(1)}, u32[]{:S(2)}, u32[]{:S(2)}) collective-permute-start(bf16[4,1,80,128]{3,2,1,0:T(8,128)(2,1)} %get-tuple-element.32), channel_id=1, source_target_pairs={{0,1},{1,2},{2,3},{3,4},{4,5},{5,6},{6,7},{7,8},{8,9},{9,10},{10,1... | collective-permute-start | bytes 245768 | tf_op jit(solution)/shard_map/ppermute | solution.py:25
  48.5 6.0 %collective-permute-start.7 = (bf16[4,1,80,128]{3,2,1,0:T(8,128)(2,1)}, bf16[4,1,80,128]{3,2,1,0:T(8,128)(2,1)S(1)}, u32[]{:S(2)}, u32[]{:S(2)}) collective-permute-start(bf16[4,1,80,128]{3,2,1,0:T(8,128)(2,1)} %copy-done.10), channel_id=1, source_target_pairs={{1,0},{2,1},{3,2},{4,3},{5,4},{6,5},{7,6},{8,7},{9,8},{10,9},{11,1... | collective-permute-start | bytes 245768 | tf_op jit(solution)/shard_map/ppermute | solution.py:25
  54.5 5.0 %collective-permute-done.6.top = bf16[4,1,80,128]{3,2,1,0:T(8,128)(2,1)S(1)} collective-permute-done((bf16[4,1,80,128]{3,2,1,0:T(8,128)(2,1)}, bf16[4,1,80,128]{3,2,1,0:T(8,128)(2,1)S(1)}, u32[]{:S(2)}, u32[]{:S(2)}) %collective-permute-start.6) | collective-permute-done | bytes 81952 | tf_op jit(solution)/shard_map/ppermute | solution.py:25
  59.8 23.1 %all_to_all.15.parts_ref = f32[8,56,128]{2,1,0:T(8,128)S(1)} all-to-all(f32[8,56,128]{2,1,0:T(8,128)S(1)} %add_chips.1), channel_id=1, replica_groups=mesh['xl'=2,'z1'=4,'z0'=4,'y'=4,'xh'=2,'co'=2] {'xl','z0'}, dimensions={0} | all-to-all | bytes 458752 | tf_op jit(solution)/shard_map/all_to_all | solution.py:364
  82.9 8.3 %collective-permute-start.8 = (f32[56,128]{1,0:T(8,128)S(1)}, f32[56,128]{1,0:T(8,128)S(1)}, u32[]{:S(2)}, u32[]{:S(2)}) collective-permute-start(f32[56,128]{1,0:T(8,128)S(1)} %add_parts.1.own_ref), channel_id=1, source_target_pairs={{0,128},{1,129},{2,130},{3,131},{4,132},{5,133},{6,134},{7,135},{8... | collective-permute-start | bytes 86024 | tf_op jit(solution)/shard_map/ppermute | solution.py:25
  91.2 9.4 %collective-permute-start.10 = (f32[56,128]{1,0:T(8,128)S(1)}, f32[56,128]{1,0:T(8,128)S(1)}, u32[]{:S(2)}, u32[]{:S(2)}) collective-permute-start(f32[56,128]{1,0:T(8,128)S(1)} %add_parts.1.own_ref), channel_id=1, source_target_pairs={{0,192},{1,193},{2,194},{3,195},{4,196},{5,197},{6,198},{7,199},{8... | collective-permute-start | bytes 86024 | tf_op jit(solution)/shard_map/ppermute | solution.py:25
  100.5 7.3 %collective-permute-start.9 = (f32[56,128]{1,0:T(8,128)S(1)}, f32[56,128]{1,0:T(8,128)S(1)}, u32[]{:S(2)}, u32[]{:S(2)}) collective-permute-start(f32[56,128]{1,0:T(8,128)S(1)} %add_parts.1.own_ref), channel_id=1, source_target_pairs={{0,64},{1,65},{2,66},{3,67},{4,68},{5,69},{6,70},{7,71},{8,72},{9,... | collective-permute-start | bytes 86024 | tf_op jit(solution)/shard_map/ppermute | solution.py:25
  107.9 1.5 %copy-done.5 = bf16[3456,256]{1,0:T(8,128)(2,1)S(1)} copy-done((bf16[3456,256]{1,0:T(8,128)(2,1)S(1)}, bf16[3456,256]{1,0:T(8,128)(2,1)}, u32[]{:S(2)}) %copy-start.5) | copy-done | bytes 1769496
  109.3 1.2 copy-done.7
  110.5 8.1 %outputs.1 = (bf16[2,8,80,256]{3,2,1,0:T(8,128)(2,1)}, bf16[2,8,80,128]{3,2,1,0:T(8,128)(2,1)}) custom-call(bf16[16,216,256]{2,1,0:T(8,128)(2,1)S(1)} %bitcast.2, bf16[2,8,80,384]{3,2,1,0:T(8,128)(2,1)S(1)} %copy-done.7, bf16[2,8,80,384]{3,2,1,0:T(8,128)(2,1)S(1)} %get-tuple-element.25.act.own_act, bf16[4,1,80,128]{3,2,1,0:T(8,128)(2,1)S(1)} %collective-permute-done.6.top, ...), custom_call_target="tpu_custom_call" | custom-call | flops 4529848320 | bytes 8388608 | tf_op jit(solution)/shard_map/outputs/pallas_call | solution.py:323
  118.7 10.7 %all_to_all.16.whole_ref = f32[8,56,128]{2,1,0:T(8,128)S(1)} all-to-all(f32[8,56,128]{2,1,0:T(8,128)S(1)} %add_far.1), channel_id=1, replica_groups=mesh['xl'=2,'z1'=4,'z0'=4,'y'=4,'xh'=2,'co'=2] {'xl','z0'}, dimensions={0} | all-to-all | bytes 458752 | tf_op jit(solution)/shard_map/all_to_all | solution.py:380
  129.4 0.7 finish.1
  (29 shorter events, 0.4 us)
Async XLA Ops:
  7.2 100.7 %all-gather.3.cloned.1.call-start = ((), (), s32[]{:S(2)}) async-start(), calls=%async_computation.3 | async-start | bytes 1880064 | tf_op jit(solution)/shard_map/all_gather | solution.py:349
  7.9 21.4 %collective-permute-start.1 = (bf16[2,8,80,256]{3,2,1,0:T(8,128)(2,1)}, bf16[2,8,80,256]{3,2,1,0:T(8,128)(2,1)}, u32[]{:S(2)}, u32[]{:S(2)}) collective-permute-start(bf16[2,8,80,256]{3,2,1,0:T(8,128)(2,1)} %cot.1), channel_id=1, source_target_pairs={{16,0},{17,1},{18,2},{19,3},{20,4},{21,5},{22,6},{23,7},{24,8},{25... | collective-permute-start | bytes 1966088 | tf_op jit(solution)/shard_map/ppermute | solution.py:25
  9.2 20.1 %collective-permute-start = (bf16[2,8,80,128]{3,2,1,0:T(8,128)(2,1)}, bf16[2,8,80,128]{3,2,1,0:T(8,128)(2,1)S(1)}, u32[]{:S(2)}, u32[]{:S(2)}) collective-permute-start(bf16[2,8,80,128]{3,2,1,0:T(8,128)(2,1)} %own.3), channel_id=1, source_target_pairs={{0,16},{1,17},{2,18},{3,19},{4,20},{5,21},{6,22},{7,23},{8,24},{9,... | collective-permute-start | bytes 983048 | tf_op jit(solution)/shard_map/ppermute | solution.py:25
  14.7 12.1 %collective-permute-start.2 = (bf16[2,1,80,256]{3,2,1,0:T(8,128)(2,1)S(1)}, bf16[2,1,80,256]{3,2,1,0:T(8,128)(2,1)S(1)}, u32[]{:S(2)}, u32[]{:S(2)}) collective-permute-start(bf16[2,1,80,256]{3,2,1,0:T(8,128)(2,1)S(1)} %get-tuple-element.46), channel_id=1, source_target_pairs={{0,1},{1,2},{2,3},{3,4},{4,5},{5,6},{6,7},{7,8},{8,9},{9,10},{10,1... | collective-permute-start | bytes 245768 | tf_op jit(solution)/shard_map/ppermute | solution.py:25
  16.7 10.1 %collective-permute-start.3 = (bf16[2,1,80,256]{3,2,1,0:T(8,128)(2,1)S(1)}, bf16[2,1,80,256]{3,2,1,0:T(8,128)(2,1)S(1)}, u32[]{:S(2)}, u32[]{:S(2)}) collective-permute-start(bf16[2,1,80,256]{3,2,1,0:T(8,128)(2,1)S(1)} %get-tuple-element.45), channel_id=1, source_target_pairs={{1,0},{2,1},{3,2},{4,3},{5,4},{6,5},{7,6},{8,7},{9,8},{10,9},{11,1... | collective-permute-start | bytes 245768 | tf_op jit(solution)/shard_map/ppermute | solution.py:25
  22.7 1.1 copy-start
  23.8 1.0 copy-start.1
  24.8 0.7 copy-start.3
  25.4 3.9 %copy-start.4 = (f32[128]{0:T(128)S(1)}, f32[128]{0:T(128)}, u32[]{:S(2)}) copy-start(f32[128]{0:T(128)} %gain.5) | copy-start | bytes 1540
  25.9 0.8 copy-start.8
  26.8 1.1 copy-start.9
  32.2 1.0 copy-start.6
  33.1 12.1 %copy-start.10 = (bf16[4,1,80,128]{3,2,1,0:T(8,128)(2,1)}, bf16[4,1,80,128]{3,2,1,0:T(8,128)(2,1)S(1)}, u32[]{:S(2)}) copy-start(bf16[4,1,80,128]{3,2,1,0:T(8,128)(2,1)S(1)} %get-tuple-element.33) | copy-start | bytes 245764
  33.1 4.4 %collective-permute-start.4 = (bf16[8,224,256]{2,1,0:T(8,128)(2,1)S(1)}, bf16[8,224,256]{2,1,0:T(8,128)(2,1)S(1)}, u32[]{:S(2)}, u32[]{:S(2)}) collective-permute-start(bf16[8,224,256]{2,1,0:T(8,128)(2,1)S(1)} %get-tuple-element.30), channel_id=1, source_target_pairs={{0,1},{1,0},{2,3},{3,2},{4,5},{5,4},{6,7},{7,6},{8,9},{9,8},{10,11... | collective-permute-start | bytes 2752520 | tf_op jit(solution)/shard_map/ppermute | solution.py:25
  38.6 69.2 %copy-start.2 = (bf16[2,8,80,128]{3,2,1,0:T(8,128)(2,1)S(1)}, bf16[2,8,80,128]{3,2,1,0:T(8,128)(2,1)}, u32[]{:S(2)}) copy-start(bf16[2,8,80,128]{3,2,1,0:T(8,128)(2,1)} %own.3) | copy-start | bytes 983044
  38.6 21.0 %all-to-all-start = ((bf16[8,224,256]{2,1,0:T(8,128)(2,1)}), bf16[8,224,256]{2,1,0:T(8,128)(2,1)S(1)}, u32[]{:S(2)}, u32[]{:S(2)}) async-start(bf16[8,224,256]{2,1,0:T(8,128)(2,1)} %add_cores.1), calls=%async_computation | async-start | bytes 1835008 | tf_op jit(solution)/shard_map/all_to_all | solution.py:359
  45.3 9.3 %collective-permute-start.5 = (bf16[2,2,80,256]{3,2,1,0:T(8,128)(2,1)S(1)}, bf16[2,2,80,256]{3,2,1,0:T(8,128)(2,1)S(1)}, u32[]{:S(2)}, u32[]{:S(2)}) collective-permute-start(bf16[2,2,80,256]{3,2,1,0:T(8,128)(2,1)S(1)} %get-tuple-element.31), channel_id=1, source_target_pairs={{16,0},{17,1},{18,2},{19,3},{20,4},{21,5},{22,6},{23,7},{24,8},{25... | collective-permute-start | bytes 491528 | tf_op jit(solution)/shard_map/ppermute | solution.py:25
  46.6 13.0 %collective-permute-start.6 = (bf16[4,1,80,128]{3,2,1,0:T(8,128)(2,1)}, bf16[4,1,80,128]{3,2,1,0:T(8,128)(2,1)S(1)}, u32[]{:S(2)}, u32[]{:S(2)}) collective-permute-start(bf16[4,1,80,128]{3,2,1,0:T(8,128)(2,1)} %get-tuple-element.32), channel_id=1, source_target_pairs={{0,1},{1,2},{2,3},{3,4},{4,5},{5,6},{6,7},{7,8},{8,9},{9,10},{10,1... | collective-permute-start | bytes 245768 | tf_op jit(solution)/shard_map/ppermute | solution.py:25
  48.5 11.1 %collective-permute-start.7 = (bf16[4,1,80,128]{3,2,1,0:T(8,128)(2,1)}, bf16[4,1,80,128]{3,2,1,0:T(8,128)(2,1)S(1)}, u32[]{:S(2)}, u32[]{:S(2)}) collective-permute-start(bf16[4,1,80,128]{3,2,1,0:T(8,128)(2,1)} %copy-done.10), channel_id=1, source_target_pairs={{1,0},{2,1},{3,2},{4,3},{5,4},{6,5},{7,6},{8,7},{9,8},{10,9},{11,1... | collective-permute-start | bytes 245768 | tf_op jit(solution)/shard_map/ppermute | solution.py:25
  82.9 35.7 %collective-permute-start.8 = (f32[56,128]{1,0:T(8,128)S(1)}, f32[56,128]{1,0:T(8,128)S(1)}, u32[]{:S(2)}, u32[]{:S(2)}) collective-permute-start(f32[56,128]{1,0:T(8,128)S(1)} %add_parts.1.own_ref), channel_id=1, source_target_pairs={{0,128},{1,129},{2,130},{3,131},{4,132},{5,133},{6,134},{7,135},{8... | collective-permute-start | bytes 86024 | tf_op jit(solution)/shard_map/ppermute | solution.py:25
  91.2 27.5 %collective-permute-start.10 = (f32[56,128]{1,0:T(8,128)S(1)}, f32[56,128]{1,0:T(8,128)S(1)}, u32[]{:S(2)}, u32[]{:S(2)}) collective-permute-start(f32[56,128]{1,0:T(8,128)S(1)} %add_parts.1.own_ref), channel_id=1, source_target_pairs={{0,192},{1,193},{2,194},{3,195},{4,196},{5,197},{6,198},{7,199},{8... | collective-permute-start | bytes 86024 | tf_op jit(solution)/shard_map/ppermute | solution.py:25
  100.5 18.1 %collective-permute-start.9 = (f32[56,128]{1,0:T(8,128)S(1)}, f32[56,128]{1,0:T(8,128)S(1)}, u32[]{:S(2)}, u32[]{:S(2)}) collective-permute-start(f32[56,128]{1,0:T(8,128)S(1)} %add_parts.1.own_ref), channel_id=1, source_target_pairs={{0,64},{1,65},{2,66},{3,67},{4,68},{5,69},{6,70},{7,71},{8,72},{9,... | collective-permute-start | bytes 86024 | tf_op jit(solution)/shard_map/ppermute | solution.py:25
  107.9 1.5 %copy-start.5 = (bf16[3456,256]{1,0:T(8,128)(2,1)S(1)}, bf16[3456,256]{1,0:T(8,128)(2,1)}, u32[]{:S(2)}) copy-start(bf16[3456,256]{1,0:T(8,128)(2,1)} %all-gather.3.cloned.1.call-done) | copy-start | bytes 5308420
  109.3 1.2 copy-start.7
Sparse Core Ops, SparseCore 0:
  11.3 66.0 all-gather.2

commit v2 on v1

v2 whole, which is shorter than its diff:
```python
import jax
import jax.numpy as jnp
from jax import lax
from jax.experimental import pallas as pl
from jax.experimental.pallas import tpu as pltpu
from jax.sharding import Mesh, PartitionSpec as P

epsilon = 1e-06
F32 = jnp.float32
BF16 = jnp.bfloat16
TM = ("xl", "z1", "z0")
SPACE = ("y", "xh", "co")
SIZES = (2, 4, 4, 4, 2, 2)
AXES = TM + SPACE
TMS, SPACES = 32, 16


def shift(block, target):
    route = []
    for t in range(TMS):
        for s in range(SPACES):
            u, v = target(t, s)
            if 0 <= u < TMS and 0 <= v < SPACES:
                route.append((t * SPACES + s, u * SPACES + v))
    return lax.ppermute(block, AXES, route)


def beside(block):
    cols = block.shape[1]
    col = lax.broadcasted_iota(jnp.int32, block.shape, 1)
    left = jnp.where(col == 0, 0.0, pltpu.roll(block, 1, 1))
    right = jnp.where(col == cols - 1, 0.0, pltpu.roll(block, cols - 1, 1))
    return jnp.concatenate([left, block, right], axis=-1).astype(BF16)


def activated(block, gain):
    frames, rows, cols, channels = block.shape
    v = block.reshape(frames * rows, cols, channels).astype(F32)
    z = v * lax.rsqrt(jnp.mean(v * v, axis=-1, keepdims=True) + epsilon) * gain
    return z / (1.0 + jnp.exp(-z))


def gradient(act, pad):
    frames = act.shape[0]
    rows = act.reshape(frames * 640, 384)
    shifted = [pad[:, 2 - b : 10 - b].reshape(frames * 640, 256) for b in range(3)]
    return lax.dot_general(
        rows,
        jnp.concatenate(shifted, axis=-1),
        (((0,), (0,)), ((), ())),
        preferred_element_type=F32,
    )


def kernel_grad_body(
    core, prev, own, gain, cot, top, low, cot_edges, row_edges, keep, send, act, pad, part, total
):
    g = gain[...].reshape(1, 1, 128)
    act[2:4] = beside(activated(own[...], g)).reshape(2, 8, 80, 384)
    act[0:2] = beside(activated(prev[...], g)).reshape(2, 8, 80, 384)
    for index, outer in enumerate((top, low)):
        row_edges[:, index : index + 1] = outer[:, :, :, :128]
        cot_edges[:, index : index + 1] = outer[:, :, :, 128:]
        pad[:, 9 * index : 9 * index + 1] = outer[:, :, :, 128:]
    pad[:, 1:9] = cot[...]
    for a in range(3):
        part_of = total.at[a] if a < 2 else part
        part_of[...] = gradient(act[a : a + 2], pad[...])

    def tap(index):
        a, b, e = index // 9, index // 3 % 3, index % 3
        ref = part if a == 2 else total.at[a]
        return ref, 128 * e, 256 * b

    def pack(even, odd):
        for pair in range(14):
            for chip in range(8):
                for out, parity in ((even, 0), (odd, 1)):
                    blocks = []
                    for index in (2 * pair, min(2 * pair + 1, 26)):
                        ref, row, col = tap(index)
                        row = row + 16 * chip + 8 * parity
                        blocks.append(ref[row : row + 8, col : col + 256])
                    if pair == 13:
                        blocks[1] = jnp.zeros_like(blocks[1])
                    both = jnp.concatenate(blocks, axis=0).astype(BF16)
                    out[chip, 16 * pair : 16 * pair + 16] = both

    @pl.when(core[0] == 0)
    def _():
        pack(keep, send)

    @pl.when(core[0] != 0)
    def _():
        pack(send, keep)


VMEM = pl.BlockSpec(memory_space=pltpu.VMEM)
SMEM = pl.BlockSpec(memory_space=pltpu.SMEM)
ANY = pl.BlockSpec(memory_space=pl.ANY)


def kernel_gradient(core, prev, own, gain, cot, top, low):
    return pl.pallas_call(
        kernel_grad_body,
        out_shape=(
            jax.ShapeDtypeStruct((2, 2, 80, 256), BF16),
            jax.ShapeDtypeStruct((2, 2, 80, 128), BF16),
            jax.ShapeDtypeStruct((8, 224, 256), BF16),
            jax.ShapeDtypeStruct((8, 224, 256), BF16),
        ),
        in_specs=[SMEM] + [VMEM] * 6,
        out_specs=(VMEM,) * 4,
        scratch_shapes=[
            pltpu.VMEM((4, 8, 80, 384), BF16),
            pltpu.VMEM((2, 10, 80, 256), BF16),
            pltpu.VMEM((384, 768), F32),
            pltpu.VMEM((2, 384, 768), F32),
        ],
        compiler_params=pltpu.CompilerParams(vmem_limit_bytes=20 << 20),
        cost_estimate=pl.CostEstimate(
            flops=2 * 1280 * 3456 * 256, bytes_accessed=6 << 20, transcendentals=1 << 18
        ),
        name="kernel_grad",
    )(core, prev, own, gain, cot, top, low)


def call(body, name, out_shape, args, specs=None, scratch=()):
    return pl.pallas_call(
        body,
        out_shape=out_shape,
        in_specs=specs or [VMEM] * len(args),
        out_specs=VMEM,
        scratch_shapes=scratch,
        compiler_params=pltpu.CompilerParams(vmem_limit_bytes=6 << 20),
        name=name,
    )(*args)


def add_cores(keep, got):
    def body(keep_ref, got_ref, out_ref):
        out_ref[...] = (keep_ref[...].astype(F32) + got_ref[...].astype(F32)).astype(BF16)

    shape = jax.ShapeDtypeStruct(keep.shape, BF16)
    return call(body, "add_cores", shape, (keep, got))


def add_chips(rows):
    def body(rows_ref, out_ref):
        total = rows_ref[0].astype(F32)
        for chip in range(1, 8):
            total = total + rows_ref[chip].astype(F32)
        for side in range(2):
            for quarter in range(4):
                block = total[56 * quarter : 56 * quarter + 56, 128 * side : 128 * side + 128]
                out_ref[4 * side + quarter] = block

    shape = jax.ShapeDtypeStruct((8, 56, 128), F32)
    return call(body, "add_chips", shape, (rows,))


def add_parts(parts, copies):
    shape = (copies, *parts.shape[1:])

    def body(parts_ref, out_ref):
        total = parts_ref[0]
        for index in range(1, parts.shape[0]):
            total = total + parts_ref[index]
        out_ref[...] = jnp.broadcast_to(total, shape)

    return call(body, "add_parts", jax.ShapeDtypeStruct(shape, F32), (parts,))


def repeat(rows, copies):
    shape = (copies, *rows.shape)

    def body(rows_ref, out_ref):
        for index in range(copies):
            out_ref[index] = rows_ref[...]

    return call(body, "repeat", jax.ShapeDtypeStruct(shape, rows.dtype), (rows,))


def finish(whole):
    def body(whole_ref, out_ref, side_ref):
        for side in range(2):
            for tap in range(27):
                row = 8 * tap
                block = whole_ref[4 * side + row // 56, row % 56 : row % 56 + 8]
                side_ref[side, pl.ds(tap, 8, stride=27), :] = block
            out_ref[:, 128 * side : 128 * side + 128] = side_ref[side]

    shape = jax.ShapeDtypeStruct((216, 256), F32)
    scratch = (pltpu.VMEM((2, 216, 128), F32),)
    return call(body, "finish", shape, (whole,), None, scratch)


def decode_body(
    core,
    mine_hbm,
    other_hbm,
    prev_hbm,
    own_hbm,
    gain,
    dec_hbm,
    kern_hbm,
    kern,
    raw,
    act,
    mine,
    other,
    prev,
    own,
    dec,
    sems,
):
    pairs = ((mine_hbm, mine), (other_hbm, other), (prev_hbm, prev), (own_hbm, own))
    loads = [
        pltpu.make_async_copy(source, held, sems.at[index])
        for index, (source, held) in enumerate(pairs)
    ]
    for load in loads:
        load.start()
    loads[0].wait()
    loads[1].wait()
    for chip in range(8):
        for side in range(2):
            columns = slice(128 * side, 128 * side + 128)
            one, two = [ref[chip, :, columns].astype(F32) for ref in (mine, other)]
            raw[side, 0] = jnp.where(core[0] == 0, one, two)
            raw[side, 1] = jnp.where(core[0] == 0, two, one)
            for tap in range(27):
                rows = [raw[side, half, pl.ds(tap, 8, stride=27), :] for half in range(2)]
                rows = jnp.concatenate(rows, axis=0).astype(BF16)
                kern[tap, 16 * chip : 16 * chip + 16, columns] = rows
    stores = [pltpu.make_async_copy(kern, kern_hbm, sems.at[4])]
    stores[0].start()
    loads[2].wait()
    loads[3].wait()
    g = gain[...].reshape(1, 1, 128)
    act[0:2] = beside(activated(prev[...], g)).reshape(2, 8, 80, 384)
    act[2:4] = beside(activated(own[...], g)).reshape(2, 8, 80, 384)
    for t in range(2):
        for half in range(2):
            at = 3 * half
            patches = [
                act[t + a, at + b : at + b + 3].reshape(240, 384)
                for a in range(3)
                for b in range(3)
            ]
            out = jnp.dot(
                jnp.concatenate(patches, axis=-1),
                kern[...].reshape(3456, 256),
                preferred_element_type=F32,
            )
            dec[t, at : at + 3] = out.astype(BF16).reshape(3, 80, 256)
            stores.append(
                pltpu.make_async_copy(
                    dec.at[t, at : at + 3],
                    dec_hbm.at[t, at + 1 : at + 4],
                    sems.at[5 + 2 * t + half],
                )
            )
            stores[-1].start()
    for store in stores:
        store.wait()


def decode(core, mine, other, prev, own, gain):
    return pl.pallas_call(
        decode_body,
        out_shape=(
            jax.ShapeDtypeStruct((2, 8, 80, 256), BF16),
            jax.ShapeDtypeStruct((27, 128, 256), BF16),
        ),
        in_specs=[SMEM] + [ANY] * 4 + [VMEM],
        out_specs=(ANY, ANY),
        scratch_shapes=[
            pltpu.VMEM((27, 128, 256), BF16),
            pltpu.VMEM((2, 2, 216, 128), F32),
            pltpu.VMEM((4, 8, 80, 384), BF16),
            pltpu.VMEM((8, 216, 256), BF16),
            pltpu.VMEM((8, 216, 256), BF16),
            pltpu.VMEM((2, 8, 80, 128), BF16),
            pltpu.VMEM((2, 8, 80, 128), BF16),
            pltpu.VMEM((2, 6, 80, 256), BF16),
            pltpu.SemaphoreType.DMA((9,)),
        ],
        compiler_params=pltpu.CompilerParams(vmem_limit_bytes=60 << 20),
        cost_estimate=pl.CostEstimate(
            flops=2 * 1280 * 3456 * 256, bytes_accessed=8 << 20, transcendentals=0
        ),
        name="decode",
    )(core, mine, other, prev, own, gain)


def finish_outputs_body(
    kern_hbm,
    prev_hbm,
    own_hbm,
    prev_edges,
    own_edges,
    cot_hbm,
    edges,
    next_cot_hbm,
    next_edges,
    gain,
    inner,
    dec,
    ing,
    act,
    rows_out,
    kern,
    prev,
    own,
    cot,
    next_cot,
    sems,
):
    pairs = (
        (own_hbm, own),
        (prev_hbm, prev),
        (kern_hbm, kern),
        (cot_hbm, cot),
        (next_cot_hbm, next_cot),
    )
    loads = [
        pltpu.make_async_copy(source, held, sems.at[4 + index])
        for index, (source, held) in enumerate(pairs)
    ]
    for load in loads:
        load.start()
    g = gain[...].reshape(1, 1, 128)
    loads[0].wait()
    loads[1].wait()
    for index, at in enumerate((0, 6)):
        first = 1 - index
        sources = ((prev, prev_edges), (own, own_edges))
        for frames, (block, outer) in enumerate(sources):
            at_frames = slice(2 * frames, 2 * frames + 2)
            act[at_frames, first : first + 2] = beside(
                activated(block[:, at : at + 2], g)
            ).reshape(2, 2, 80, 384)
            act[at_frames, 2 * index : 2 * index + 1] = beside(
                activated(outer[:, index : index + 1], g)
            ).reshape(2, 1, 80, 384)
        if index == 0:
            loads[2].wait()
        patches = [
            act[a : a + 2, b].reshape(160, 384) for a in range(3) for b in range(3)
        ]
        out = jnp.dot(
            jnp.concatenate(patches, axis=-1),
            kern[...].reshape(3456, 256),
            preferred_element_type=F32,
        )
        rows_out[index] = out.astype(BF16).reshape(2, 80, 256)
    copies = [
        pltpu.make_async_copy(
            rows_out.at[index, t], dec.at[t, 7 * index], sems.at[2 * index + t]
        )
        for index in range(2)
        for t in range(2)
    ]
    for copy in copies:
        copy.start()
    loads[3].wait()
    loads[4].wait()

    def cot_rows(frame, at):
        ref, outer, frame = (
            (cot, edges, frame) if frame < 2 else (next_cot, next_edges, frame - 2)
        )
        if at < 0:
            rows = jnp.concatenate([outer[frame, 0:1], ref[frame, 0:3]], axis=0)
        elif at > 4:
            rows = jnp.concatenate([ref[frame, 5:8], outer[frame, 1:2]], axis=0)
        else:
            rows = ref[frame, at : at + 4]
        return rows.reshape(320, 256)

    for s in range(2):
        for half in range(2):
            sums = jnp.zeros((320, 384), F32)
            for a in range(3):
                for b in range(3):
                    window = cot_rows(s + 2 - a, 4 * half + 1 - b)
                    weights = kern[9 * a + 3 * b : 9 * a + 3 * b + 3].reshape(384, 256)
                    sums = sums + lax.dot_general(
                        window, weights, (((1,), (1,)), ((), ())), preferred_element_type=F32
                    )
            sums = sums.reshape(4, 80, 384)
            left, mid, right = sums[..., :128], sums[..., 128:256], sums[..., 256:]
            col = lax.broadcasted_iota(jnp.int32, mid.shape, 1)
            grad = mid + jnp.where(col == 79, 0.0, pltpu.roll(left, 79, 1))
            grad = grad + jnp.where(col == 0, 0.0, pltpu.roll(right, 1, 1))
            v = own[s, 4 * half : 4 * half + 4].astype(F32)
            scale = lax.rsqrt(jnp.mean(v * v, axis=-1, keepdims=True) + epsilon)
            normed = v * scale
            z = normed * g
            gate = 1.0 / (1.0 + jnp.exp(-z))
            dn = grad * (gate * (1.0 + z * (1.0 - gate))) * g
            out = scale * (dn - normed * jnp.mean(dn * normed, axis=-1, keepdims=True))
            ing[s, 4 * half : 4 * half + 4] = out.astype(BF16)
    for copy in copies:
        copy.wait()


def finish_outputs(
    kern, prev, own, prev_edges, own_edges, cot, edges, next_cot, next_edges, gain, inner
):
    return pl.pallas_call(
        finish_outputs_body,
        out_shape=(
            jax.ShapeDtypeStruct((2, 8, 80, 256), BF16),
            jax.ShapeDtypeStruct((2, 8, 80, 128), BF16),
        ),
        in_specs=[ANY] * 3 + [VMEM] * 2 + [ANY, VMEM, ANY, VMEM, VMEM, ANY],
        out_specs=(ANY, VMEM),
        input_output_aliases={10: 0},
        scratch_shapes=[
            pltpu.VMEM((4, 3, 80, 384), BF16),
            pltpu.VMEM((2, 2, 80, 256), BF16),
            pltpu.VMEM((27, 128, 256), BF16),
            pltpu.VMEM((2, 8, 80, 128), BF16),
            pltpu.VMEM((2, 8, 80, 128), BF16),
            pltpu.VMEM((2, 8, 80, 256), BF16),
            pltpu.VMEM((2, 8, 80, 256), BF16),
            pltpu.SemaphoreType.DMA((9,)),
        ],
        compiler_params=pltpu.CompilerParams(vmem_limit_bytes=60 << 20),
        cost_estimate=pl.CostEstimate(
            flops=2 * 1280 * 3456 * 256, bytes_accessed=8 << 20, transcendentals=1 << 18
        ),
        name="finish_outputs",
    )(kern, prev, own, prev_edges, own_edges, cot, edges, next_cot, next_edges, gain, inner)


def on_device(features, norm_gain, kernel, cotangent):
    core = lax.axis_index("co").reshape(1)
    tie = lax.optimization_barrier
    next_cot = shift(cotangent, lambda t, s: (t - 1, s))
    prev = shift(features, lambda t, s: (t + 1, s))
    last = jnp.concatenate([features[:, 7:], cotangent[:, 7:]], axis=-1)
    first = jnp.concatenate([features[:, :1], cotangent[:, :1]], axis=-1)
    top = shift(last, lambda t, s: (t, s + 1))
    low = shift(first, lambda t, s: (t, s - 1))
    next_cot, prev, top, low, repeated = tie((next_cot, prev, top, low, repeat(kernel, 8)))
    mine = lax.all_to_all(repeated, ("y", "xh"), 0, 0, tiled=True)
    edges, own_edges, keep, send = kernel_gradient(
        core, prev, features, norm_gain, cotangent, top, low
    )
    next_edges = shift(edges, lambda t, s: (t - 1, s))
    prev_edges = shift(own_edges, lambda t, s: (t + 1, s))
    keep, mine = tie((keep, mine))
    other = shift(mine, lambda t, s: (t, s ^ 1))
    both = add_cores(keep, shift(send, lambda t, s: (t, s ^ 1)))
    rows = lax.all_to_all(both, ("y", "xh"), 0, 0, tiled=True)
    inner, kern = decode(core, mine, other, prev, features, norm_gain)
    rows, inner, prev_edges, next_edges = tie((rows, inner, prev_edges, next_edges))
    parts = lax.all_to_all(add_chips(rows), ("xl", "z0"), 0, 0, tiled=True)
    parts = lax.all_to_all(add_parts(parts, 4), "z1", 0, 0, tiled=True)
    decoded, input_grad = finish_outputs(
        kern,
        prev,
        features,
        prev_edges,
        own_edges,
        cotangent,
        edges,
        next_cot,
        next_edges,
        norm_gain,
        inner,
    )
    parts, decoded, input_grad = tie((parts, decoded, input_grad))
    whole = lax.all_to_all(add_parts(parts, 8), ("xl", "z0"), 0, 0, tiled=True)
    return (decoded, finish(whole), input_grad)


def solution(mesh):
    fine = Mesh(mesh.devices.reshape(SIZES), AXES)
    split = P(TM, SPACE, None, None)
    rows = P(SPACE, None)
    return jax.shard_map(
        on_device,
        mesh=fine,
        in_specs=(split, P(), rows, split),
        out_specs=(split, rows, split),
        check_vma=False,
    )
```

time: 138 us -> 124 us (0.90)
  the two profiles are of different devices: /device:TPU:8 before, /device:TPU:2 now
where the time goes in v2:
time: 124 us; the launch traced here: 123 us
  starting transfers between devices  54.7 us (44%)
  blocking collectives  22.3 us (18%)
  Pallas kernels  21.2 us (17%)
  waiting for transfers between devices  20.3 us (16%)
  local copies, waits for them, and re-layouts  3.7 us (3%)
    ppermute x8, starting transfers between devices, shift(): return lax.ppermute(block, AXES, route)  31.2 us
    all_to_all x1, starting transfers between devices, on_device(): parts = lax.all_to_all(add_parts(parts, 4), 'z1', 0, 0, tiled=True)  13.6 us
    all_to_all x1, blocking collectives, on_device(): parts = lax.all_to_all(add_chips(rows), ('xl', 'z0'), 0, 0, tiled=True)  11.5 us
    all_to_all x1, blocking collectives, on_device(): whole = lax.all_to_all(add_parts(parts, 8), ('xl', 'z0'), 0, 0, tiled=True)  10.9 us
    all_to_all x1, waiting for transfers between devices, on_device(): mine = lax.all_to_all(repeated, ('y', 'xh'), 0, 0, tiled=True)  8.4 us
    pallas_call x1, Pallas kernels, finish_outputs(): pl.pallas_call(finish_outputs_body, out_shape=(jax.ShapeDtypeStruct((2, 8...  7.75 us
    all_to_all x1, starting transfers between devices, on_device(): mine = lax.all_to_all(repeated, ('y', 'xh'), 0, 0, tiled=True)  6.33 us
    ppermute x8, waiting for transfers between devices, shift(): return lax.ppermute(block, AXES, route)  5.79 us
  transfers between devices with their start and end apart: 11, of which 6 were waited for; matrix products, arithmetic and copies ran while one was open for 2% of the time, Pallas kernels for 16%

profile of v2, /device:TPU:2, one launch (start us, length us, event | category | flops | bytes accessed | tf_op | source)
XLA Modules:
  0.0 123.1 jit_solution(17286577289153720975)
XLA Ops:
  0.6 11.4 %collective-permute-start = (bf16[2,8,80,256]{3,2,1,0:T(8,128)(2,1)}, bf16[2,8,80,256]{3,2,1,0:T(8,128)(2,1)S(1)}, u32[]{:S(2)}, u32[]{:S(2)}) collective-permute-start(bf16[2,8,80,256]{3,2,1,0:T(8,128)(2,1)} %cot_hbm.1), channel_id=1, source_target_pairs={{16,0},{17,1},{18,2},{19,3},{20,4},{21,5},{22,6},{23,7},{24,8},{25... | collective-permute-start | bytes 1966088 | tf_op jit(solution)/shard_map/ppermute | solution.py:25
  12.0 1.9 %collective-permute-start.1 = (bf16[2,8,80,128]{3,2,1,0:T(8,128)(2,1)}, bf16[2,8,80,128]{3,2,1,0:T(8,128)(2,1)S(1)}, u32[]{:S(2)}, u32[]{:S(2)}) collective-permute-start(bf16[2,8,80,128]{3,2,1,0:T(8,128)(2,1)} %own_hbm.3), channel_id=1, source_target_pairs={{0,16},{1,17},{2,18},{3,19},{4,20},{5,21},{6,22},{7,23},{8,24},{9,... | collective-permute-start | bytes 983048 | tf_op jit(solution)/shard_map/ppermute | solution.py:25
  14.0 0.9 fusion.1
  14.8 1.0 fusion
  15.9 1.5 %collective-permute-start.2 = (bf16[2,1,80,384]{3,2,1,0:T(8,128)(2,1)S(1)}, bf16[2,1,80,384]{3,2,1,0:T(8,128)(2,1)S(1)}, u32[]{:S(2)}, u32[]{:S(2)}) collective-permute-start(bf16[2,1,80,384]{3,2,1,0:T(8,128)(2,1)S(1)} %pad_maximum_fusion), channel_id=1, source_target_pairs={{0,1},{1,2},{2,3},{3,4},{4,5},{5,6},{6,7},{7,8},{8,9},{9,10},{10,1... | collective-permute-start | bytes 368648 | tf_op jit(solution)/shard_map/ppermute | solution.py:25
  17.4 1.3 %collective-permute-start.3 = (bf16[2,1,80,384]{3,2,1,0:T(8,128)(2,1)S(1)}, bf16[2,1,80,384]{3,2,1,0:T(8,128)(2,1)S(1)}, u32[]{:S(2)}, u32[]{:S(2)}) collective-permute-start(bf16[2,1,80,384]{3,2,1,0:T(8,128)(2,1)S(1)} %pad_maximum_fusion.1), channel_id=1, source_target_pairs={{1,0},{2,1},{3,2},{4,3},{5,4},{6,5},{7,6},{8,7},{9,8},{10,9},{11,1... | collective-permute-start | bytes 368648 | tf_op jit(solution)/shard_map/ppermute | solution.py:25
  18.7 0.0 copy-start
  18.7 0.9 copy-done
  19.6 1.0 repeat.1
  20.6 2.5 %collective-permute-done.3.low = bf16[2,1,80,384]{3,2,1,0:T(8,128)(2,1)S(1)} collective-permute-done((bf16[2,1,80,384]{3,2,1,0:T(8,128)(2,1)S(1)}, bf16[2,1,80,384]{3,2,1,0:T(8,128)(2,1)S(1)}, u32[]{:S(2)}, u32[]{:S(2)}) %collective-permute-start.3) | collective-permute-done | bytes 122912 | tf_op jit(solution)/shard_map/ppermute | solution.py:25
  23.1 2.3 %collective-permute-done.1.prev.prev_hbm = bf16[2,8,80,128]{3,2,1,0:T(8,128)(2,1)S(1)} collective-permute-done((bf16[2,8,80,128]{3,2,1,0:T(8,128)(2,1)}, bf16[2,8,80,128]{3,2,1,0:T(8,128)(2,1)S(1)}, u32[]{:S(2)}, u32[]{:S(2)}) %collective-permute-start.1) | collective-permute-done | bytes 327712 | tf_op jit(solution)/shard_map/ppermute | solution.py:25
  25.4 0.9 collective-permute-done.next_cot_hbm
  26.3 6.3 %all-to-all-start = ((bf16[8,216,256]{2,1,0:T(8,128)(2,1)}), bf16[8,216,256]{2,1,0:T(8,128)(2,1)}, u32[]{:S(2)}, u32[]{:S(2)}) async-start(bf16[8,216,256]{2,1,0:T(8,128)(2,1)} %repeat.1), calls=%async_computation | async-start | bytes 1769472 | tf_op jit(solution)/shard_map/all_to_all | solution.py:449
  32.7 4.1 %kernel_grad.1 = (bf16[2,2,80,256]{3,2,1,0:T(8,128)(2,1)S(1)}, bf16[2,2,80,128]{3,2,1,0:T(8,128)(2,1)S(1)}, bf16[8,224,256]{2,1,0:T(8,128)(2,1)S(1)}, bf16[8,224,256]{2,1,0:T(8,128)(2,1)}) custom-call(s32[1]{0:T(128)} %bitcast.core, bf16[2,8,80,128]{3,2,1,0:T(8,128)(2,1)S(1)} %collective-permute-done.1.prev.prev_hbm, bf16[2,8,80,128]{3,2,1,0:T(8,128)(2,1)S(1)} %copy-done.2, ...), custom_call_target="tpu_custom_call" | custom-call | flops 2264924160 | bytes 6291456 | tf_op jit(solution)/shard_map/kernel_grad/pallas_call | solution.py:104
  36.8 3.7 %collective-permute-start.4 = (bf16[8,224,256]{2,1,0:T(8,128)(2,1)}, bf16[8,224,256]{2,1,0:T(8,128)(2,1)S(1)}, u32[]{:S(2)}, u32[]{:S(2)}) collective-permute-start(bf16[8,224,256]{2,1,0:T(8,128)(2,1)} %get-tuple-element.31), channel_id=1, source_target_pairs={{0,1},{1,0},{2,3},{3,2},{4,5},{5,4},{6,7},{7,6},{8,9},{9,8},{10,11... | collective-permute-start | bytes 2752520 | tf_op jit(solution)/shard_map/ppermute | solution.py:25
  40.5 8.4 %all-to-all-done.mine_hbm = bf16[8,216,256]{2,1,0:T(8,128)(2,1)} async-done(((bf16[8,216,256]{2,1,0:T(8,128)(2,1)}), bf16[8,216,256]{2,1,0:T(8,128)(2,1)}, u32[]{:S(2)}, u32[]{:S(2)}) %all-to-all-start) | async-done | bytes 884768 | tf_op jit(solution)/shard_map/all_to_all | solution.py:449
  48.9 2.5 %collective-permute-start.5 = (bf16[8,216,256]{2,1,0:T(8,128)(2,1)}, bf16[8,216,256]{2,1,0:T(8,128)(2,1)S(1)}, u32[]{:S(2)}, u32[]{:S(2)}) collective-permute-start(bf16[8,216,256]{2,1,0:T(8,128)(2,1)} %all-to-all-done.mine_hbm), channel_id=1, source_target_pairs={{0,1},{1,0},{2,3},{3,2},{4,5},{5,4},{6,7},{7,6},{8,9},{9,8},{10,11... | collective-permute-start | bytes 2654216 | tf_op jit(solution)/shard_map/ppermute | solution.py:25
  51.4 1.2 add_cores.1
  52.5 3.6 %all-to-all-start.1 = ((bf16[8,224,256]{2,1,0:T(8,128)(2,1)}), bf16[8,224,256]{2,1,0:T(8,128)(2,1)S(1)}, u32[]{:S(2)}, u32[]{:S(2)}) async-start(bf16[8,224,256]{2,1,0:T(8,128)(2,1)} %add_cores.1), calls=%async_computation.1 | async-start | bytes 1835008 | tf_op jit(solution)/shard_map/all_to_all | solution.py:458
  56.1 1.9 %collective-permute-start.6 = (bf16[2,2,80,128]{3,2,1,0:T(8,128)(2,1)S(1)}, bf16[2,2,80,128]{3,2,1,0:T(8,128)(2,1)S(1)}, u32[]{:S(2)}, u32[]{:S(2)}) collective-permute-start(bf16[2,2,80,128]{3,2,1,0:T(8,128)(2,1)S(1)} %get-tuple-element.34.own_edges), channel_id=1, source_target_pairs={{0,16},{1,17},{2,18},{3,19},{4,20},{5,21},{6,22},{7,23},{8,24},{9,... | collective-permute-start | bytes 245768 | tf_op jit(solution)/shard_map/ppermute | solution.py:25
  58.0 7.0 %collective-permute-start.7 = (bf16[2,2,80,256]{3,2,1,0:T(8,128)(2,1)S(1)}, bf16[2,2,80,256]{3,2,1,0:T(8,128)(2,1)S(1)}, u32[]{:S(2)}, u32[]{:S(2)}) collective-permute-start(bf16[2,2,80,256]{3,2,1,0:T(8,128)(2,1)S(1)} %get-tuple-element.35.edges), channel_id=1, source_target_pairs={{16,0},{17,1},{18,2},{19,3},{20,4},{21,5},{22,6},{23,7},{24,8},{25... | collective-permute-start | bytes 491528 | tf_op jit(solution)/shard_map/ppermute | solution.py:25
  65.1 0.9 copy-done.7
  66.0 5.7 %decode.1 = (bf16[2,8,80,256]{3,2,1,0:T(8,128)(2,1)}, bf16[27,128,256]{2,1,0:T(8,128)(2,1)}) custom-call(s32[1]{0:T(128)} %bitcast.core, bf16[8,216,256]{2,1,0:T(8,128)(2,1)} %all-to-all-done.mine_hbm, bf16[8,216,256]{2,1,0:T(8,128)(2,1)} %copy-done.7, bf16[2,8,80,128]{3,2,1,0:T(8,128)(2,1)} %copy-done.3, bf16[2,8,80,128]{3,2,1,0:T(8,128)(2,1)} %own_hbm.3, ...), custom_call_target="tpu_custom_call" | custom-call | flops 2264924160 | bytes 8388608 | tf_op jit(solution)/shard_map/decode/pallas_call | solution.py:270
  71.8 0.5 all-to-all-done.1.rows_ref
  72.3 0.1 add_chips.1
  72.4 11.5 %all_to_all.25.parts_ref = f32[8,56,128]{2,1,0:T(8,128)S(1)} all-to-all(f32[8,56,128]{2,1,0:T(8,128)S(1)} %add_chips.1), channel_id=1, replica_groups=mesh['xl'=2,'z1'=4,'z0'=4,'y'=4,'xh'=2,'co'=2] {'xl','z0'}, dimensions={0} | all-to-all | bytes 458752 | tf_op jit(solution)/shard_map/all_to_all | solution.py:461
  83.9 0.7 add_parts.2
  84.5 13.6 %all-to-all-start.3 = ((f32[4,56,128]{2,1,0:T(8,128)}), f32[4,56,128]{2,1,0:T(8,128)S(1)}, u32[]{:S(2)}, u32[]{:S(2)}) async-start(f32[4,56,128]{2,1,0:T(8,128)} %add_parts.2), calls=%async_computation.3 | async-start | bytes 229376 | tf_op jit(solution)/shard_map/all_to_all | solution.py:462
  98.1 7.7 %finish_outputs.1 = (bf16[2,8,80,256]{3,2,1,0:T(8,128)(2,1)}, bf16[2,8,80,128]{3,2,1,0:T(8,128)(2,1)}) custom-call(bf16[27,128,256]{2,1,0:T(8,128)(2,1)} %get-tuple-element.37.kern_hbm, bf16[2,8,80,128]{3,2,1,0:T(8,128)(2,1)} %copy-done.3, bf16[2,8,80,128]{3,2,1,0:T(8,128)(2,1)} %own_hbm.3, ...), custom_call_target="tpu_custom_call", output_to_operand_aliasing={{0}: (10, {})} | custom-call | flops 2264924160 | bytes 8388608 | tf_op jit(solution)/shard_map/finish_outputs/pallas_call | solution.py:412
  105.9 5.6 %all-to-all-done.3.parts_ref = f32[4,56,128]{2,1,0:T(8,128)S(1)} async-done(((f32[4,56,128]{2,1,0:T(8,128)}), f32[4,56,128]{2,1,0:T(8,128)S(1)}, u32[]{:S(2)}, u32[]{:S(2)}) %all-to-all-start.3) | async-done | bytes 114720 | tf_op jit(solution)/shard_map/all_to_all | solution.py:462
  111.6 10.9 %all_to_all.26.whole_ref = f32[8,56,128]{2,1,0:T(8,128)S(1)} all-to-all(f32[8,56,128]{2,1,0:T(8,128)S(1)} %add_parts.3), channel_id=1, replica_groups=mesh['xl'=2,'z1'=4,'z0'=4,'y'=4,'xh'=2,'co'=2] {'xl','z0'}, dimensions={0} | all-to-all | bytes 458752 | tf_op jit(solution)/shard_map/all_to_all | solution.py:477
  122.4 0.7 finish.1
  (27 shorter events, 0.1 us)
Async XLA Ops:
  0.6 25.7 %collective-permute-start = (bf16[2,8,80,256]{3,2,1,0:T(8,128)(2,1)}, bf16[2,8,80,256]{3,2,1,0:T(8,128)(2,1)S(1)}, u32[]{:S(2)}, u32[]{:S(2)}) collective-permute-start(bf16[2,8,80,256]{3,2,1,0:T(8,128)(2,1)} %cot_hbm.1), channel_id=1, source_target_pairs={{16,0},{17,1},{18,2},{19,3},{20,4},{21,5},{22,6},{23,7},{24,8},{25... | collective-permute-start | bytes 1966088 | tf_op jit(solution)/shard_map/ppermute | solution.py:25
  12.0 13.4 %collective-permute-start.1 = (bf16[2,8,80,128]{3,2,1,0:T(8,128)(2,1)}, bf16[2,8,80,128]{3,2,1,0:T(8,128)(2,1)S(1)}, u32[]{:S(2)}, u32[]{:S(2)}) collective-permute-start(bf16[2,8,80,128]{3,2,1,0:T(8,128)(2,1)} %own_hbm.3), channel_id=1, source_target_pairs={{0,16},{1,17},{2,18},{3,19},{4,20},{5,21},{6,22},{7,23},{8,24},{9,... | collective-permute-start | bytes 983048 | tf_op jit(solution)/shard_map/ppermute | solution.py:25
  13.9 18.7 %copy-start.2 = (bf16[2,8,80,128]{3,2,1,0:T(8,128)(2,1)S(1)}, bf16[2,8,80,128]{3,2,1,0:T(8,128)(2,1)}, u32[]{:S(2)}) copy-start(bf16[2,8,80,128]{3,2,1,0:T(8,128)(2,1)} %own_hbm.3) | copy-start | bytes 983044
  14.8 17.9 %copy-start.1 = (bf16[2,8,80,256]{3,2,1,0:T(8,128)(2,1)S(1)}, bf16[2,8,80,256]{3,2,1,0:T(8,128)(2,1)}, u32[]{:S(2)}) copy-start(bf16[2,8,80,256]{3,2,1,0:T(8,128)(2,1)} %cot_hbm.1) | copy-start | bytes 1966084
  14.8 17.9 %copy-start.6 = (f32[128]{0:T(128)S(1)}, f32[128]{0:T(128)}, u32[]{:S(2)}) copy-start(f32[128]{0:T(128)} %gain.5) | copy-start | bytes 1540
  15.9 4.7 %collective-permute-start.2 = (bf16[2,1,80,384]{3,2,1,0:T(8,128)(2,1)S(1)}, bf16[2,1,80,384]{3,2,1,0:T(8,128)(2,1)S(1)}, u32[]{:S(2)}, u32[]{:S(2)}) collective-permute-start(bf16[2,1,80,384]{3,2,1,0:T(8,128)(2,1)S(1)} %pad_maximum_fusion), channel_id=1, source_target_pairs={{0,1},{1,2},{2,3},{3,4},{4,5},{5,6},{6,7},{7,8},{8,9},{9,10},{10,1... | collective-permute-start | bytes 368648 | tf_op jit(solution)/shard_map/ppermute | solution.py:25
  17.4 5.7 %collective-permute-start.3 = (bf16[2,1,80,384]{3,2,1,0:T(8,128)(2,1)S(1)}, bf16[2,1,80,384]{3,2,1,0:T(8,128)(2,1)S(1)}, u32[]{:S(2)}, u32[]{:S(2)}) collective-permute-start(bf16[2,1,80,384]{3,2,1,0:T(8,128)(2,1)S(1)} %pad_maximum_fusion.1), channel_id=1, source_target_pairs={{1,0},{2,1},{3,2},{4,3},{5,4},{6,5},{7,6},{8,7},{9,8},{10,9},{11,1... | collective-permute-start | bytes 368648 | tf_op jit(solution)/shard_map/ppermute | solution.py:25
  18.7 0.9 copy-start
  25.4 11.4 %copy-start.3 = (bf16[2,8,80,128]{3,2,1,0:T(8,128)(2,1)}, bf16[2,8,80,128]{3,2,1,0:T(8,128)(2,1)S(1)}, u32[]{:S(2)}) copy-start(bf16[2,8,80,128]{3,2,1,0:T(8,128)(2,1)S(1)} %collective-permute-done.1.prev.prev_hbm) | copy-start | bytes 983044
  26.3 6.3 %copy-start.8 = (bf16[2,8,80,256]{3,2,1,0:T(8,128)(2,1)}, bf16[2,8,80,256]{3,2,1,0:T(8,128)(2,1)S(1)}, u32[]{:S(2)}) copy-start(bf16[2,8,80,256]{3,2,1,0:T(8,128)(2,1)S(1)} %collective-permute-done.next_cot_hbm) | copy-start | bytes 1966084
  26.3 22.5 %all-to-all-start = ((bf16[8,216,256]{2,1,0:T(8,128)(2,1)}), bf16[8,216,256]{2,1,0:T(8,128)(2,1)}, u32[]{:S(2)}, u32[]{:S(2)}) async-start(bf16[8,216,256]{2,1,0:T(8,128)(2,1)} %repeat.1), calls=%async_computation | async-start | bytes 1769472 | tf_op jit(solution)/shard_map/all_to_all | solution.py:449
  36.8 19.3 %copy-start.5 = (bf16[2,2,80,128]{3,2,1,0:T(8,128)(2,1)}, bf16[2,2,80,128]{3,2,1,0:T(8,128)(2,1)S(1)}, u32[]{:S(2)}) copy-start(bf16[2,2,80,128]{3,2,1,0:T(8,128)(2,1)S(1)} %get-tuple-element.34.own_edges) | copy-start | bytes 245764
  36.8 21.3 %copy-start.4 = (bf16[2,2,80,256]{3,2,1,0:T(8,128)(2,1)}, bf16[2,2,80,256]{3,2,1,0:T(8,128)(2,1)S(1)}, u32[]{:S(2)}) copy-start(bf16[2,2,80,256]{3,2,1,0:T(8,128)(2,1)S(1)} %get-tuple-element.35.edges) | copy-start | bytes 491524
  36.8 14.6 %collective-permute-start.4 = (bf16[8,224,256]{2,1,0:T(8,128)(2,1)}, bf16[8,224,256]{2,1,0:T(8,128)(2,1)S(1)}, u32[]{:S(2)}, u32[]{:S(2)}) collective-permute-start(bf16[8,224,256]{2,1,0:T(8,128)(2,1)} %get-tuple-element.31), channel_id=1, source_target_pairs={{0,1},{1,0},{2,3},{3,2},{4,5},{5,4},{6,7},{7,6},{8,9},{9,8},{10,11... | collective-permute-start | bytes 2752520 | tf_op jit(solution)/shard_map/ppermute | solution.py:25
  48.9 16.2 %collective-permute-start.5 = (bf16[8,216,256]{2,1,0:T(8,128)(2,1)}, bf16[8,216,256]{2,1,0:T(8,128)(2,1)S(1)}, u32[]{:S(2)}, u32[]{:S(2)}) collective-permute-start(bf16[8,216,256]{2,1,0:T(8,128)(2,1)} %all-to-all-done.mine_hbm), channel_id=1, source_target_pairs={{0,1},{1,0},{2,3},{3,2},{4,5},{5,4},{6,7},{7,6},{8,9},{9,8},{10,11... | collective-permute-start | bytes 2654216 | tf_op jit(solution)/shard_map/ppermute | solution.py:25
  52.5 19.8 %all-to-all-start.1 = ((bf16[8,224,256]{2,1,0:T(8,128)(2,1)}), bf16[8,224,256]{2,1,0:T(8,128)(2,1)S(1)}, u32[]{:S(2)}, u32[]{:S(2)}) async-start(bf16[8,224,256]{2,1,0:T(8,128)(2,1)} %add_cores.1), calls=%async_computation.1 | async-start | bytes 1835008 | tf_op jit(solution)/shard_map/all_to_all | solution.py:458
  56.1 15.6 %collective-permute-start.6 = (bf16[2,2,80,128]{3,2,1,0:T(8,128)(2,1)S(1)}, bf16[2,2,80,128]{3,2,1,0:T(8,128)(2,1)S(1)}, u32[]{:S(2)}, u32[]{:S(2)}) collective-permute-start(bf16[2,2,80,128]{3,2,1,0:T(8,128)(2,1)S(1)} %get-tuple-element.34.own_edges), channel_id=1, source_target_pairs={{0,16},{1,17},{2,18},{3,19},{4,20},{5,21},{6,22},{7,23},{8,24},{9,... | collective-permute-start | bytes 245768 | tf_op jit(solution)/shard_map/ppermute | solution.py:25
  58.0 13.7 %collective-permute-start.7 = (bf16[2,2,80,256]{3,2,1,0:T(8,128)(2,1)S(1)}, bf16[2,2,80,256]{3,2,1,0:T(8,128)(2,1)S(1)}, u32[]{:S(2)}, u32[]{:S(2)}) collective-permute-start(bf16[2,2,80,256]{3,2,1,0:T(8,128)(2,1)S(1)} %get-tuple-element.35.edges), channel_id=1, source_target_pairs={{16,0},{17,1},{18,2},{19,3},{20,4},{21,5},{22,6},{23,7},{24,8},{25... | collective-permute-start | bytes 491528 | tf_op jit(solution)/shard_map/ppermute | solution.py:25
  65.1 0.9 copy-start.7
  71.7 26.4 %copy-start.10 = (bf16[2,2,80,128]{3,2,1,0:T(8,128)(2,1)}, bf16[2,2,80,128]{3,2,1,0:T(8,128)(2,1)S(1)}, u32[]{:S(2)}) copy-start(bf16[2,2,80,128]{3,2,1,0:T(8,128)(2,1)S(1)} %collective-permute-done.6.prev_edges) | copy-start | bytes 245764
  71.7 26.4 %copy-start.9 = (bf16[2,2,80,256]{3,2,1,0:T(8,128)(2,1)}, bf16[2,2,80,256]{3,2,1,0:T(8,128)(2,1)S(1)}, u32[]{:S(2)}) copy-start(bf16[2,2,80,256]{3,2,1,0:T(8,128)(2,1)S(1)} %collective-permute-done.7.next_edges) | copy-start | bytes 491524
  84.5 27.0 %all-to-all-start.3 = ((f32[4,56,128]{2,1,0:T(8,128)}), f32[4,56,128]{2,1,0:T(8,128)S(1)}, u32[]{:S(2)}, u32[]{:S(2)}) async-start(f32[4,56,128]{2,1,0:T(8,128)} %add_parts.2), calls=%async_computation.3 | async-start | bytes 229376 | tf_op jit(solution)/shard_map/all_to_all | solution.py:462

commit v3 on v2

--- a/solution.py
+++ b/solution.py
@@ -201,6 +201,8 @@
     other_hbm,
     prev_hbm,
     own_hbm,
+    prev_edges,
+    own_edges,
     gain,
     dec_hbm,
     kern_hbm,
@@ -238,13 +240,17 @@
     loads[2].wait()
     loads[3].wait()
     g = gain[...].reshape(1, 1, 128)
-    act[0:2] = beside(activated(prev[...], g)).reshape(2, 8, 80, 384)
-    act[2:4] = beside(activated(own[...], g)).reshape(2, 8, 80, 384)
+    for frame, block, outer in ((0, prev, prev_edges), (2, own, own_edges)):
+        frames = slice(frame, frame + 2)
+        act[frames, 1:9] = beside(activated(block[...], g)).reshape(2, 8, 80, 384)
+        edge = beside(activated(outer[...], g)).reshape(2, 2, 80, 384)
+        act[frames, 0:1] = edge[:, 0:1]
+        act[frames, 9:10] = edge[:, 1:2]
     for t in range(2):
         for half in range(2):
-            at = 3 * half
+            at = 4 * half
             patches = [
-                act[t + a, at + b : at + b + 3].reshape(240, 384)
+                act[t + a, at + b : at + b + 4].reshape(320, 384)
                 for a in range(3)
                 for b in range(3)
             ]
@@ -253,12 +259,10 @@
                 kern[...].reshape(3456, 256),
                 preferred_element_type=F32,
             )
-            dec[t, at : at + 3] = out.astype(BF16).reshape(3, 80, 256)
+            dec[t, at : at + 4] = out.astype(BF16).reshape(4, 80, 256)
             stores.append(
                 pltpu.make_async_copy(
-                    dec.at[t, at : at + 3],
-                    dec_hbm.at[t, at + 1 : at + 4],
-                    sems.at[5 + 2 * t + half],
+                    dec.at[t, at : at + 4], dec_hbm.at[t, at : at + 4], sems.at[5 + 2 * t + half]
                 )
             )
             stores[-1].start()
@@ -266,24 +270,24 @@
         store.wait()
 
 
-def decode(core, mine, other, prev, own, gain):
+def decode(core, mine, other, prev, own, prev_edges, own_edges, gain):
     return pl.pallas_call(
         decode_body,
         out_shape=(
             jax.ShapeDtypeStruct((2, 8, 80, 256), BF16),
             jax.ShapeDtypeStruct((27, 128, 256), BF16),
         ),
-        in_specs=[SMEM] + [ANY] * 4 + [VMEM],
+        in_specs=[SMEM] + [ANY] * 4 + [VMEM] * 3,
         out_specs=(ANY, ANY),
         scratch_shapes=[
             pltpu.VMEM((27, 128, 256), BF16),
             pltpu.VMEM((2, 2, 216, 128), F32),
-            pltpu.VMEM((4, 8, 80, 384), BF16),
+            pltpu.VMEM((4, 10, 80, 384), BF16),
             pltpu.VMEM((8, 216, 256), BF16),
             pltpu.VMEM((8, 216, 256), BF16),
             pltpu.VMEM((2, 8, 80, 128), BF16),
             pltpu.VMEM((2, 8, 80, 128), BF16),
-            pltpu.VMEM((2, 6, 80, 256), BF16),
+            pltpu.VMEM((2, 8, 80, 256), BF16),
             pltpu.SemaphoreType.DMA((9,)),
         ],
         compiler_params=pltpu.CompilerParams(vmem_limit_bytes=60 << 20),
@@ -291,81 +295,36 @@
             flops=2 * 1280 * 3456 * 256, bytes_accessed=8 << 20, transcendentals=0
         ),
         name="decode",
-    )(core, mine, other, prev, own, gain)
-
-
-def finish_outputs_body(
+    )(core, mine, other, prev, own, prev_edges, own_edges, gain)
+
+
+def input_grad_body(
     kern_hbm,
-    prev_hbm,
     own_hbm,
-    prev_edges,
-    own_edges,
     cot_hbm,
     edges,
     next_cot_hbm,
     next_edges,
     gain,
-    inner,
-    dec,
     ing,
-    act,
-    rows_out,
     kern,
-    prev,
     own,
     cot,
     next_cot,
     sems,
 ):
-    pairs = (
-        (own_hbm, own),
-        (prev_hbm, prev),
-        (kern_hbm, kern),
-        (cot_hbm, cot),
-        (next_cot_hbm, next_cot),
-    )
+    pairs = [(cot_hbm, cot), (next_cot_hbm, next_cot), (own_hbm, own)]
+    for a in range(3):
+        taps = slice(9 * a, 9 * a + 9)
+        pairs.append((kern_hbm.at[taps], kern.at[taps]))
     loads = [
-        pltpu.make_async_copy(source, held, sems.at[4 + index])
+        pltpu.make_async_copy(source, held, sems.at[index])
         for index, (source, held) in enumerate(pairs)
     ]
-    for load in loads:
-        load.start()
+    for index in (0, 5, 4, 1, 3, 2):
+        loads[index].start()
     g = gain[...].reshape(1, 1, 128)
     loads[0].wait()
-    loads[1].wait()
-    for index, at in enumerate((0, 6)):
-        first = 1 - index
-        sources = ((prev, prev_edges), (own, own_edges))
-        for frames, (block, outer) in enumerate(sources):
-            at_frames = slice(2 * frames, 2 * frames + 2)
-            act[at_frames, first : first + 2] = beside(
-                activated(block[:, at : at + 2], g)
-            ).reshape(2, 2, 80, 384)
-            act[at_frames, 2 * index : 2 * index + 1] = beside(
-                activated(outer[:, index : index + 1], g)
-            ).reshape(2, 1, 80, 384)
-        if index == 0:
-            loads[2].wait()
-        patches = [
-            act[a : a + 2, b].reshape(160, 384) for a in range(3) for b in range(3)
-        ]
-        out = jnp.dot(
-            jnp.concatenate(patches, axis=-1),
-            kern[...].reshape(3456, 256),
-            preferred_element_type=F32,
-        )
-        rows_out[index] = out.astype(BF16).reshape(2, 80, 256)
-    copies = [
-        pltpu.make_async_copy(
-            rows_out.at[index, t], dec.at[t, 7 * index], sems.at[2 * index + t]
-        )
-        for index in range(2)
-        for t in range(2)
-    ]
-    for copy in copies:
-        copy.start()
-    loads[3].wait()
-    loads[4].wait()
 
     def cot_rows(frame, at):
         ref, outer, frame = (
@@ -382,7 +341,11 @@
     for s in range(2):
         for half in range(2):
             sums = jnp.zeros((320, 384), F32)
-            for a in range(3):
+            for a in (2, 1, 0):
+                if s == 0 and half == 0:
+                    loads[3 + a].wait()
+                    if a == 0:
+                        loads[1].wait()
                 for b in range(3):
                     window = cot_rows(s + 2 - a, 4 * half + 1 - b)
                     weights = kern[9 * a + 3 * b : 9 * a + 3 * b + 3].reshape(384, 256)
@@ -394,6 +357,8 @@
             col = lax.broadcasted_iota(jnp.int32, mid.shape, 1)
             grad = mid + jnp.where(col == 79, 0.0, pltpu.roll(left, 79, 1))
             grad = grad + jnp.where(col == 0, 0.0, pltpu.roll(right, 1, 1))
+            if s == 0 and half == 0:
+                loads[2].wait()
             v = own[s, 4 * half : 4 * half + 4].astype(F32)
             scale = lax.rsqrt(jnp.mean(v * v, axis=-1, keepdims=True) + epsilon)
             normed = v * scale
@@ -402,38 +367,27 @@
             dn = grad * (gate * (1.0 + z * (1.0 - gate))) * g
             out = scale * (dn - normed * jnp.mean(dn * normed, axis=-1, keepdims=True))
             ing[s, 4 * half : 4 * half + 4] = out.astype(BF16)
-    for copy in copies:
-        copy.wait()
-
-
-def finish_outputs(
-    kern, prev, own, prev_edges, own_edges, cot, edges, next_cot, next_edges, gain, inner
-):
+
+
+def input_gradient(kern, own, cot, edges, next_cot, next_edges, gain):
     return pl.pallas_call(
-        finish_outputs_body,
-        out_shape=(
-            jax.ShapeDtypeStruct((2, 8, 80, 256), BF16),
-            jax.ShapeDtypeStruct((2, 8, 80, 128), BF16),
-        ),
-        in_specs=[ANY] * 3 + [VMEM] * 2 + [ANY, VMEM, ANY, VMEM, VMEM, ANY],
-        out_specs=(ANY, VMEM),
-        input_output_aliases={10: 0},
+        input_grad_body,
+        out_shape=jax.ShapeDtypeStruct((2, 8, 80, 128), BF16),
+        in_specs=[ANY] * 3 + [VMEM, ANY, VMEM, VMEM],
+        out_specs=VMEM,
         scratch_shapes=[
-            pltpu.VMEM((4, 3, 80, 384), BF16),
-            pltpu.VMEM((2, 2, 80, 256), BF16),
             pltpu.VMEM((27, 128, 256), BF16),
-            pltpu.VMEM((2, 8, 80, 128), BF16),
             pltpu.VMEM((2, 8, 80, 128), BF16),
             pltpu.VMEM((2, 8, 80, 256), BF16),
             pltpu.VMEM((2, 8, 80, 256), BF16),
-            pltpu.SemaphoreType.DMA((9,)),
+            pltpu.SemaphoreType.DMA((6,)),
         ],
         compiler_params=pltpu.CompilerParams(vmem_limit_bytes=60 << 20),
         cost_estimate=pl.CostEstimate(
             flops=2 * 1280 * 3456 * 256, bytes_accessed=8 << 20, transcendentals=1 << 18
         ),
-        name="finish_outputs",
-    )(kern, prev, own, prev_edges, own_edges, cot, edges, next_cot, next_edges, gain, inner)
+        name="input_grad",
+    )(kern, own, cot, edges, next_cot, next_edges, gain)
 
 
 def on_device(features, norm_gain, kernel, cotangent):
@@ -452,28 +406,20 @@
     )
     next_edges = shift(edges, lambda t, s: (t - 1, s))
     prev_edges = shift(own_edges, lambda t, s: (t + 1, s))
-    keep, mine = tie((keep, mine))
+    keep, mine, prev_edges = tie((keep, mine, prev_edges))
     other = shift(mine, lambda t, s: (t, s ^ 1))
     both = add_cores(keep, shift(send, lambda t, s: (t, s ^ 1)))
     rows = lax.all_to_all(both, ("y", "xh"), 0, 0, tiled=True)
-    inner, kern = decode(core, mine, other, prev, features, norm_gain)
-    rows, inner, prev_edges, next_edges = tie((rows, inner, prev_edges, next_edges))
+    decoded, kern = decode(
+        core, mine, other, prev, features, prev_edges, own_edges, norm_gain
+    )
+    rows, decoded, next_edges = tie((rows, decoded, next_edges))
     parts = lax.all_to_all(add_chips(rows), ("xl", "z0"), 0, 0, tiled=True)
     parts = lax.all_to_all(add_parts(parts, 4), "z1", 0, 0, tiled=True)
-    decoded, input_grad = finish_outputs(
-        kern,
-        prev,
-        features,
-        prev_edges,
-        own_edges,
-        cotangent,
-        edges,
-        next_cot,
-        next_edges,
-        norm_gain,
-        inner,
+    input_grad = input_gradient(
+        kern, features, cotangent, edges, next_cot, next_edges, norm_gain
     )
-    parts, decoded, input_grad = tie((parts, decoded, input_grad))
+    parts, input_grad = tie((parts, input_grad))
     whole = lax.all_to_all(add_parts(parts, 8), ("xl", "z0"), 0, 0, tiled=True)
     return (decoded, finish(whole), input_grad)
 

time: 124 us -> 123 us (level)
  waiting for transfers between devices: 20.3 us -> 23.8 us
  starting transfers between devices: 54.7 us -> 52 us
  blocking collectives: 22.3 us -> 21 us
    all_to_all x1, waiting for transfers between devices: 8.4 us -> 0.01 us  [on_device(): mine = lax.all_to_all(repeated, ('y', 'xh'), 0, 0, tiled=True)]
    ppermute x8, waiting for transfers between devices: 5.79 us -> 12.5 us  [shift(): return lax.ppermute(block, AXES, route)]
    all_to_all x1, waiting for transfers between devices: 0.52 us -> 4.64 us  [on_device(): rows = lax.all_to_all(both, ('y', 'xh'), 0, 0, tiled=True)]
    ppermute x8, starting transfers between devices: 31.2 us -> 28.1 us  [shift(): return lax.ppermute(block, AXES, route)]
    all_to_all x1, starting transfers between devices: 3.55 us -> 6.41 us  [on_device(): rows = lax.all_to_all(both, ('y', 'xh'), 0, 0, tiled=True)]
    all_to_all x1, starting transfers between devices: 13.6 us -> 11.2 us  [on_device(): parts = lax.all_to_all(add_parts(parts, 4), 'z1', 0, 0, tiled=True)]
where the time goes in v3:
time: 123 us
  starting transfers between devices  52 us (42%)
  waiting for transfers between devices  23.8 us (19%)
  Pallas kernels  21.1 us (17%)
  blocking collectives  21 us (17%)
  local copies, waits for them, and re-layouts  3.71 us (3%)
    ppermute x8, starting transfers between devices, shift(): return lax.ppermute(block, AXES, route)  28.1 us
    ppermute x8, waiting for transfers between devices, shift(): return lax.ppermute(block, AXES, route)  12.5 us
    all_to_all x1, starting transfers between devices, on_device(): parts = lax.all_to_all(add_parts(parts, 4), 'z1', 0, 0, tiled=True)  11.2 us
    all_to_all x1, blocking collectives, on_device(): parts = lax.all_to_all(add_chips(rows), ('xl', 'z0'), 0, 0, tiled=True)  10.5 us
    all_to_all x1, blocking collectives, on_device(): whole = lax.all_to_all(add_parts(parts, 8), ('xl', 'z0'), 0, 0, tiled=True)  10.5 us
    pallas_call x1, Pallas kernels, input_gradient(): pl.pallas_call(input_grad_body, out_shape=jax.ShapeDtypeStruct((2, 8, 80,...  6.71 us
    all_to_all x1, waiting for transfers between devices, on_device(): parts = lax.all_to_all(add_parts(parts, 4), 'z1', 0, 0, tiled=True)  6.69 us
    pallas_call x1, Pallas kernels, decode(): pl.pallas_call(decode_body, out_shape=(jax.ShapeDtypeStruct((2, 8, 80, 25...  6.67 us
  transfers between devices with their start and end apart: 11, of which 6 were waited for; matrix products, arithmetic and copies ran while one was open for 2% of the time, Pallas kernels for 16%

profile of v3, /device:TPU:2, one launch (start us, length us, event | category | flops | bytes accessed | tf_op | source)
XLA Modules:
  0.0 122.6 jit_solution(14303258632321951741)
XLA Ops:
  0.6 11.4 %collective-permute-start = (bf16[2,8,80,256]{3,2,1,0:T(8,128)(2,1)}, bf16[2,8,80,256]{3,2,1,0:T(8,128)(2,1)S(1)}, u32[]{:S(2)}, u32[]{:S(2)}) collective-permute-start(bf16[2,8,80,256]{3,2,1,0:T(8,128)(2,1)} %cot_hbm.1), channel_id=1, source_target_pairs={{16,0},{17,1},{18,2},{19,3},{20,4},{21,5},{22,6},{23,7},{24,8},{25... | collective-permute-start | bytes 1966088 | tf_op jit(solution)/shard_map/ppermute | solution.py:25
  12.0 1.9 %collective-permute-start.1 = (bf16[2,8,80,128]{3,2,1,0:T(8,128)(2,1)}, bf16[2,8,80,128]{3,2,1,0:T(8,128)(2,1)S(1)}, u32[]{:S(2)}, u32[]{:S(2)}) collective-permute-start(bf16[2,8,80,128]{3,2,1,0:T(8,128)(2,1)} %own_hbm.3), channel_id=1, source_target_pairs={{0,16},{1,17},{2,18},{3,19},{4,20},{5,21},{6,22},{7,23},{8,24},{9,... | collective-permute-start | bytes 983048 | tf_op jit(solution)/shard_map/ppermute | solution.py:25
  13.9 0.0 copy-start.2
  14.0 0.9 fusion.1
  14.8 1.0 fusion
  15.9 1.5 %collective-permute-start.2 = (bf16[2,1,80,384]{3,2,1,0:T(8,128)(2,1)S(1)}, bf16[2,1,80,384]{3,2,1,0:T(8,128)(2,1)S(1)}, u32[]{:S(2)}, u32[]{:S(2)}) collective-permute-start(bf16[2,1,80,384]{3,2,1,0:T(8,128)(2,1)S(1)} %pad_maximum_fusion), channel_id=1, source_target_pairs={{0,1},{1,2},{2,3},{3,4},{4,5},{5,6},{6,7},{7,8},{8,9},{9,10},{10,1... | collective-permute-start | bytes 368648 | tf_op jit(solution)/shard_map/ppermute | solution.py:25
  17.4 1.3 %collective-permute-start.3 = (bf16[2,1,80,384]{3,2,1,0:T(8,128)(2,1)S(1)}, bf16[2,1,80,384]{3,2,1,0:T(8,128)(2,1)S(1)}, u32[]{:S(2)}, u32[]{:S(2)}) collective-permute-start(bf16[2,1,80,384]{3,2,1,0:T(8,128)(2,1)S(1)} %pad_maximum_fusion.1), channel_id=1, source_target_pairs={{1,0},{2,1},{3,2},{4,3},{5,4},{6,5},{7,6},{8,7},{9,8},{10,9},{11,1... | collective-permute-start | bytes 368648 | tf_op jit(solution)/shard_map/ppermute | solution.py:25
  18.7 0.9 copy-done
  19.6 1.0 repeat.1
  20.6 2.5 %collective-permute-done.3.low = bf16[2,1,80,384]{3,2,1,0:T(8,128)(2,1)S(1)} collective-permute-done((bf16[2,1,80,384]{3,2,1,0:T(8,128)(2,1)S(1)}, bf16[2,1,80,384]{3,2,1,0:T(8,128)(2,1)S(1)}, u32[]{:S(2)}, u32[]{:S(2)}) %collective-permute-start.3) | collective-permute-done | bytes 122912 | tf_op jit(solution)/shard_map/ppermute | solution.py:25
  23.1 2.3 %collective-permute-done.1.prev.prev_hbm = bf16[2,8,80,128]{3,2,1,0:T(8,128)(2,1)S(1)} collective-permute-done((bf16[2,8,80,128]{3,2,1,0:T(8,128)(2,1)}, bf16[2,8,80,128]{3,2,1,0:T(8,128)(2,1)S(1)}, u32[]{:S(2)}, u32[]{:S(2)}) %collective-permute-start.1) | collective-permute-done | bytes 327712 | tf_op jit(solution)/shard_map/ppermute | solution.py:25
  25.4 0.9 collective-permute-done.next_cot_hbm
  26.3 6.3 %all-to-all-start = ((bf16[8,216,256]{2,1,0:T(8,128)(2,1)}), bf16[8,216,256]{2,1,0:T(8,128)(2,1)}, u32[]{:S(2)}, u32[]{:S(2)}) async-start(bf16[8,216,256]{2,1,0:T(8,128)(2,1)} %repeat.1), calls=%async_computation | async-start | bytes 1769472 | tf_op jit(solution)/shard_map/all_to_all | solution.py:403
  32.7 4.1 %kernel_grad.1 = (bf16[2,2,80,256]{3,2,1,0:T(8,128)(2,1)S(1)}, bf16[2,2,80,128]{3,2,1,0:T(8,128)(2,1)S(1)}, bf16[8,224,256]{2,1,0:T(8,128)(2,1)S(1)}, bf16[8,224,256]{2,1,0:T(8,128)(2,1)}) custom-call(s32[1]{0:T(128)} %bitcast.core, bf16[2,8,80,128]{3,2,1,0:T(8,128)(2,1)S(1)} %collective-permute-done.1.prev.prev_hbm, bf16[2,8,80,128]{3,2,1,0:T(8,128)(2,1)S(1)} %copy-done.2, ...), custom_call_target="tpu_custom_call" | custom-call | flops 2264924160 | bytes 6291456 | tf_op jit(solution)/shard_map/kernel_grad/pallas_call | solution.py:104
  36.8 3.7 %collective-permute-start.5 = (bf16[8,224,256]{2,1,0:T(8,128)(2,1)}, bf16[8,224,256]{2,1,0:T(8,128)(2,1)S(1)}, u32[]{:S(2)}, u32[]{:S(2)}) collective-permute-start(bf16[8,224,256]{2,1,0:T(8,128)(2,1)} %get-tuple-element.29), channel_id=1, source_target_pairs={{0,1},{1,0},{2,3},{3,2},{4,5},{5,4},{6,7},{7,6},{8,9},{9,8},{10,11... | collective-permute-start | bytes 2752520 | tf_op jit(solution)/shard_map/ppermute | solution.py:25
  40.5 1.9 %collective-permute-start.4 = (bf16[2,2,80,128]{3,2,1,0:T(8,128)(2,1)S(1)}, bf16[2,2,80,128]{3,2,1,0:T(8,128)(2,1)S(1)}, u32[]{:S(2)}, u32[]{:S(2)}) collective-permute-start(bf16[2,2,80,128]{3,2,1,0:T(8,128)(2,1)S(1)} %get-tuple-element.27.own_edges), channel_id=1, source_target_pairs={{0,16},{1,17},{2,18},{3,19},{4,20},{5,21},{6,22},{7,23},{8,24},{9,... | collective-permute-start | bytes 245768 | tf_op jit(solution)/shard_map/ppermute | solution.py:25
  42.4 6.7 %collective-permute-done.4.prev_edges = bf16[2,2,80,128]{3,2,1,0:T(8,128)(2,1)S(1)} collective-permute-done((bf16[2,2,80,128]{3,2,1,0:T(8,128)(2,1)S(1)}, bf16[2,2,80,128]{3,2,1,0:T(8,128)(2,1)S(1)}, u32[]{:S(2)}, u32[]{:S(2)}) %collective-permute-start.4) | collective-permute-done | bytes 81952 | tf_op jit(solution)/shard_map/ppermute | solution.py:25
  49.1 2.2 %collective-permute-start.6 = (bf16[8,216,256]{2,1,0:T(8,128)(2,1)}, bf16[8,216,256]{2,1,0:T(8,128)(2,1)S(1)}, u32[]{:S(2)}, u32[]{:S(2)}) collective-permute-start(bf16[8,216,256]{2,1,0:T(8,128)(2,1)} %all-to-all-done.mine_hbm), channel_id=1, source_target_pairs={{0,1},{1,0},{2,3},{3,2},{4,5},{5,4},{6,7},{7,6},{8,9},{9,8},{10,11... | collective-permute-start | bytes 2654216 | tf_op jit(solution)/shard_map/ppermute | solution.py:25
  51.4 1.2 add_cores.1
  52.5 6.4 %all-to-all-start.1 = ((bf16[8,224,256]{2,1,0:T(8,128)(2,1)}), bf16[8,224,256]{2,1,0:T(8,128)(2,1)S(1)}, u32[]{:S(2)}, u32[]{:S(2)}) async-start(bf16[8,224,256]{2,1,0:T(8,128)(2,1)} %add_cores.1), calls=%async_computation.1 | async-start | bytes 1835008 | tf_op jit(solution)/shard_map/all_to_all | solution.py:412
  58.9 4.2 %collective-permute-start.7 = (bf16[2,2,80,256]{3,2,1,0:T(8,128)(2,1)S(1)}, bf16[2,2,80,256]{3,2,1,0:T(8,128)(2,1)S(1)}, u32[]{:S(2)}, u32[]{:S(2)}) collective-permute-start(bf16[2,2,80,256]{3,2,1,0:T(8,128)(2,1)S(1)} %get-tuple-element.33.edges), channel_id=1, source_target_pairs={{16,0},{17,1},{18,2},{19,3},{20,4},{21,5},{22,6},{23,7},{24,8},{25... | collective-permute-start | bytes 491528 | tf_op jit(solution)/shard_map/ppermute | solution.py:25
  63.2 0.9 copy-done.7
  64.1 6.7 %decode.1 = (bf16[2,8,80,256]{3,2,1,0:T(8,128)(2,1)}, bf16[27,128,256]{2,1,0:T(8,128)(2,1)}) custom-call(s32[1]{0:T(128)} %bitcast.core, bf16[8,216,256]{2,1,0:T(8,128)(2,1)} %all-to-all-done.mine_hbm, bf16[8,216,256]{2,1,0:T(8,128)(2,1)} %copy-done.7, bf16[2,8,80,128]{3,2,1,0:T(8,128)(2,1)} %copy-done.3, bf16[2,8,80,128]{3,2,1,0:T(8,128)(2,1)} %own_hbm.3, ...), custom_call_target="tpu_custom_call" | custom-call | flops 2264924160 | bytes 8388608 | tf_op jit(solution)/shard_map/decode/pallas_call | solution.py:274
  70.8 4.6 %all-to-all-done.1.rows_ref = bf16[8,224,256]{2,1,0:T(8,128)(2,1)S(1)} async-done(((bf16[8,224,256]{2,1,0:T(8,128)(2,1)}), bf16[8,224,256]{2,1,0:T(8,128)(2,1)S(1)}, u32[]{:S(2)}, u32[]{:S(2)}) %all-to-all-start.1) | async-done | bytes 917536 | tf_op jit(solution)/shard_map/all_to_all | solution.py:412
  75.4 0.1 add_chips.1
  75.5 10.5 %all_to_all.25.parts_ref = f32[8,56,128]{2,1,0:T(8,128)S(1)} all-to-all(f32[8,56,128]{2,1,0:T(8,128)S(1)} %add_chips.1), channel_id=1, replica_groups=mesh['xl'=2,'z1'=4,'z0'=4,'y'=4,'xh'=2,'co'=2] {'xl','z0'}, dimensions={0} | all-to-all | bytes 458752 | tf_op jit(solution)/shard_map/all_to_all | solution.py:417
  86.1 0.7 add_parts.2
  86.7 11.2 %all-to-all-start.3 = ((f32[4,56,128]{2,1,0:T(8,128)}), f32[4,56,128]{2,1,0:T(8,128)S(1)}, u32[]{:S(2)}, u32[]{:S(2)}) async-start(f32[4,56,128]{2,1,0:T(8,128)} %add_parts.2), calls=%async_computation.3 | async-start | bytes 229376 | tf_op jit(solution)/shard_map/all_to_all | solution.py:418
  98.0 6.7 %input_grad.1 = bf16[2,8,80,128]{3,2,1,0:T(8,128)(2,1)} custom-call(bf16[27,128,256]{2,1,0:T(8,128)(2,1)} %get-tuple-element.36.kern_hbm, bf16[2,8,80,128]{3,2,1,0:T(8,128)(2,1)} %own_hbm.3, bf16[2,8,80,256]{3,2,1,0:T(8,128)(2,1)} %cot_hbm.1, bf16[2,2,80,256]{3,2,1,0:T(8,128)(2,1)} %copy-done.4, bf16[2,8,80,256]{3,2,1,0:T(8,128)(2,1)} %copy-done.8, ...), custom_call_target="tpu_custom_call" | custom-call | flops 2264924160 | bytes 8388608 | tf_op jit(solution)/shard_map/input_grad/pallas_call | solution.py:373
  104.7 6.7 %all-to-all-done.3.parts_ref = f32[4,56,128]{2,1,0:T(8,128)S(1)} async-done(((f32[4,56,128]{2,1,0:T(8,128)}), f32[4,56,128]{2,1,0:T(8,128)S(1)}, u32[]{:S(2)}, u32[]{:S(2)}) %all-to-all-start.3) | async-done | bytes 114720 | tf_op jit(solution)/shard_map/all_to_all | solution.py:418
  111.4 10.5 %all_to_all.26.whole_ref = f32[8,56,128]{2,1,0:T(8,128)S(1)} all-to-all(f32[8,56,128]{2,1,0:T(8,128)S(1)} %add_parts.3), channel_id=1, replica_groups=mesh['xl'=2,'z1'=4,'z0'=4,'y'=4,'xh'=2,'co'=2] {'xl','z0'}, dimensions={0} | all-to-all | bytes 458752 | tf_op jit(solution)/shard_map/all_to_all | solution.py:423
  121.9 0.7 finish.1
  (27 shorter events, 0.1 us)
Async XLA Ops:
  0.6 25.7 %collective-permute-start = (bf16[2,8,80,256]{3,2,1,0:T(8,128)(2,1)}, bf16[2,8,80,256]{3,2,1,0:T(8,128)(2,1)S(1)}, u32[]{:S(2)}, u32[]{:S(2)}) collective-permute-start(bf16[2,8,80,256]{3,2,1,0:T(8,128)(2,1)} %cot_hbm.1), channel_id=1, source_target_pairs={{16,0},{17,1},{18,2},{19,3},{20,4},{21,5},{22,6},{23,7},{24,8},{25... | collective-permute-start | bytes 1966088 | tf_op jit(solution)/shard_map/ppermute | solution.py:25
  12.0 13.4 %collective-permute-start.1 = (bf16[2,8,80,128]{3,2,1,0:T(8,128)(2,1)}, bf16[2,8,80,128]{3,2,1,0:T(8,128)(2,1)S(1)}, u32[]{:S(2)}, u32[]{:S(2)}) collective-permute-start(bf16[2,8,80,128]{3,2,1,0:T(8,128)(2,1)} %own_hbm.3), channel_id=1, source_target_pairs={{0,16},{1,17},{2,18},{3,19},{4,20},{5,21},{6,22},{7,23},{8,24},{9,... | collective-permute-start | bytes 983048 | tf_op jit(solution)/shard_map/ppermute | solution.py:25
  13.9 18.7 %copy-start.2 = (bf16[2,8,80,128]{3,2,1,0:T(8,128)(2,1)S(1)}, bf16[2,8,80,128]{3,2,1,0:T(8,128)(2,1)}, u32[]{:S(2)}) copy-start(bf16[2,8,80,128]{3,2,1,0:T(8,128)(2,1)} %own_hbm.3) | copy-start | bytes 983044
  14.8 17.9 %copy-start.1 = (bf16[2,8,80,256]{3,2,1,0:T(8,128)(2,1)S(1)}, bf16[2,8,80,256]{3,2,1,0:T(8,128)(2,1)}, u32[]{:S(2)}) copy-start(bf16[2,8,80,256]{3,2,1,0:T(8,128)(2,1)} %cot_hbm.1) | copy-start | bytes 1966084
  14.8 17.9 %copy-start.6 = (f32[128]{0:T(128)S(1)}, f32[128]{0:T(128)}, u32[]{:S(2)}) copy-start(f32[128]{0:T(128)} %gain.5) | copy-start | bytes 1540
  15.9 4.7 %collective-permute-start.2 = (bf16[2,1,80,384]{3,2,1,0:T(8,128)(2,1)S(1)}, bf16[2,1,80,384]{3,2,1,0:T(8,128)(2,1)S(1)}, u32[]{:S(2)}, u32[]{:S(2)}) collective-permute-start(bf16[2,1,80,384]{3,2,1,0:T(8,128)(2,1)S(1)} %pad_maximum_fusion), channel_id=1, source_target_pairs={{0,1},{1,2},{2,3},{3,4},{4,5},{5,6},{6,7},{7,8},{8,9},{9,10},{10,1... | collective-permute-start | bytes 368648 | tf_op jit(solution)/shard_map/ppermute | solution.py:25
  17.4 5.7 %collective-permute-start.3 = (bf16[2,1,80,384]{3,2,1,0:T(8,128)(2,1)S(1)}, bf16[2,1,80,384]{3,2,1,0:T(8,128)(2,1)S(1)}, u32[]{:S(2)}, u32[]{:S(2)}) collective-permute-start(bf16[2,1,80,384]{3,2,1,0:T(8,128)(2,1)S(1)} %pad_maximum_fusion.1), channel_id=1, source_target_pairs={{1,0},{2,1},{3,2},{4,3},{5,4},{6,5},{7,6},{8,7},{9,8},{10,9},{11,1... | collective-permute-start | bytes 368648 | tf_op jit(solution)/shard_map/ppermute | solution.py:25
  18.7 0.9 copy-start
  25.4 11.4 %copy-start.3 = (bf16[2,8,80,128]{3,2,1,0:T(8,128)(2,1)}, bf16[2,8,80,128]{3,2,1,0:T(8,128)(2,1)S(1)}, u32[]{:S(2)}) copy-start(bf16[2,8,80,128]{3,2,1,0:T(8,128)(2,1)S(1)} %collective-permute-done.1.prev.prev_hbm) | copy-start | bytes 983044
  26.3 6.3 %copy-start.8 = (bf16[2,8,80,256]{3,2,1,0:T(8,128)(2,1)}, bf16[2,8,80,256]{3,2,1,0:T(8,128)(2,1)S(1)}, u32[]{:S(2)}) copy-start(bf16[2,8,80,256]{3,2,1,0:T(8,128)(2,1)S(1)} %collective-permute-done.next_cot_hbm) | copy-start | bytes 1966084
  26.3 22.8 %all-to-all-start = ((bf16[8,216,256]{2,1,0:T(8,128)(2,1)}), bf16[8,216,256]{2,1,0:T(8,128)(2,1)}, u32[]{:S(2)}, u32[]{:S(2)}) async-start(bf16[8,216,256]{2,1,0:T(8,128)(2,1)} %repeat.1), calls=%async_computation | async-start | bytes 1769472 | tf_op jit(solution)/shard_map/all_to_all | solution.py:403
  36.8 15.8 %copy-start.5 = (bf16[2,2,80,128]{3,2,1,0:T(8,128)(2,1)}, bf16[2,2,80,128]{3,2,1,0:T(8,128)(2,1)S(1)}, u32[]{:S(2)}) copy-start(bf16[2,2,80,128]{3,2,1,0:T(8,128)(2,1)S(1)} %get-tuple-element.27.own_edges) | copy-start | bytes 245764
  36.8 22.2 %copy-start.4 = (bf16[2,2,80,256]{3,2,1,0:T(8,128)(2,1)}, bf16[2,2,80,256]{3,2,1,0:T(8,128)(2,1)S(1)}, u32[]{:S(2)}) copy-start(bf16[2,2,80,256]{3,2,1,0:T(8,128)(2,1)S(1)} %get-tuple-element.33.edges) | copy-start | bytes 491524
  36.8 14.6 %collective-permute-start.5 = (bf16[8,224,256]{2,1,0:T(8,128)(2,1)}, bf16[8,224,256]{2,1,0:T(8,128)(2,1)S(1)}, u32[]{:S(2)}, u32[]{:S(2)}) collective-permute-start(bf16[8,224,256]{2,1,0:T(8,128)(2,1)} %get-tuple-element.29), channel_id=1, source_target_pairs={{0,1},{1,0},{2,3},{3,2},{4,5},{5,4},{6,7},{7,6},{8,9},{9,8},{10,11... | collective-permute-start | bytes 2752520 | tf_op jit(solution)/shard_map/ppermute | solution.py:25
  40.5 8.6 %collective-permute-start.4 = (bf16[2,2,80,128]{3,2,1,0:T(8,128)(2,1)S(1)}, bf16[2,2,80,128]{3,2,1,0:T(8,128)(2,1)S(1)}, u32[]{:S(2)}, u32[]{:S(2)}) collective-permute-start(bf16[2,2,80,128]{3,2,1,0:T(8,128)(2,1)S(1)} %get-tuple-element.27.own_edges), channel_id=1, source_target_pairs={{0,16},{1,17},{2,18},{3,19},{4,20},{5,21},{6,22},{7,23},{8,24},{9,... | collective-permute-start | bytes 245768 | tf_op jit(solution)/shard_map/ppermute | solution.py:25
  49.1 3.4 %copy-start.10 = (bf16[2,2,80,128]{3,2,1,0:T(8,128)(2,1)}, bf16[2,2,80,128]{3,2,1,0:T(8,128)(2,1)S(1)}, u32[]{:S(2)}) copy-start(bf16[2,2,80,128]{3,2,1,0:T(8,128)(2,1)S(1)} %collective-permute-done.4.prev_edges) | copy-start | bytes 245764
  49.1 14.0 %collective-permute-start.6 = (bf16[8,216,256]{2,1,0:T(8,128)(2,1)}, bf16[8,216,256]{2,1,0:T(8,128)(2,1)S(1)}, u32[]{:S(2)}, u32[]{:S(2)}) collective-permute-start(bf16[8,216,256]{2,1,0:T(8,128)(2,1)} %all-to-all-done.mine_hbm), channel_id=1, source_target_pairs={{0,1},{1,0},{2,3},{3,2},{4,5},{5,4},{6,7},{7,6},{8,9},{9,8},{10,11... | collective-permute-start | bytes 2654216 | tf_op jit(solution)/shard_map/ppermute | solution.py:25
  52.5 22.9 %all-to-all-start.1 = ((bf16[8,224,256]{2,1,0:T(8,128)(2,1)}), bf16[8,224,256]{2,1,0:T(8,128)(2,1)S(1)}, u32[]{:S(2)}, u32[]{:S(2)}) async-start(bf16[8,224,256]{2,1,0:T(8,128)(2,1)} %add_cores.1), calls=%async_computation.1 | async-start | bytes 1835008 | tf_op jit(solution)/shard_map/all_to_all | solution.py:412
  58.9 11.8 %collective-permute-start.7 = (bf16[2,2,80,256]{3,2,1,0:T(8,128)(2,1)S(1)}, bf16[2,2,80,256]{3,2,1,0:T(8,128)(2,1)S(1)}, u32[]{:S(2)}, u32[]{:S(2)}) collective-permute-start(bf16[2,2,80,256]{3,2,1,0:T(8,128)(2,1)S(1)} %get-tuple-element.33.edges), channel_id=1, source_target_pairs={{16,0},{17,1},{18,2},{19,3},{20,4},{21,5},{22,6},{23,7},{24,8},{25... | collective-permute-start | bytes 491528 | tf_op jit(solution)/shard_map/ppermute | solution.py:25
  63.1 0.9 copy-start.7
  70.8 27.2 %copy-start.9 = (bf16[2,2,80,256]{3,2,1,0:T(8,128)(2,1)}, bf16[2,2,80,256]{3,2,1,0:T(8,128)(2,1)S(1)}, u32[]{:S(2)}) copy-start(bf16[2,2,80,256]{3,2,1,0:T(8,128)(2,1)S(1)} %collective-permute-done.7.next_edges) | copy-start | bytes 491524
  86.7 24.6 %all-to-all-start.3 = ((f32[4,56,128]{2,1,0:T(8,128)}), f32[4,56,128]{2,1,0:T(8,128)S(1)}, u32[]{:S(2)}, u32[]{:S(2)}) async-start(f32[4,56,128]{2,1,0:T(8,128)} %add_parts.2), calls=%async_computation.3 | async-start | bytes 229376 | tf_op jit(solution)/shard_map/all_to_all | solution.py:418
